TPU v7x, 256 devices: a whole 4x4x8 slice. The times are simulated.
256 devices in a mesh: ctx: 16 (over y, z_lo), head: 4 (over x), dp: 4 (over z_hi, core).
Axes of the slice: x: 4, y: 4, z: 8 (z_hi: 2, z_lo: 4; z = z_hi * 4 + z_lo), core: 2. Of those that a mesh axis runs over, the one named last changes fastest.
Arguments:
- query_states: bfloat16 [32768, 8192], P(('dp', 'ctx'), 'head'), parts along dimension 0, may hold values from -6 to 6
- key_states: bfloat16 [32768, 1024], P(('dp', 'ctx'), 'head'), parts along dimension 0, may hold values from -6 to 6
- value_state_rows: bfloat16 [32768, 1024], P(('dp', 'ctx'), 'head'), parts along dimension 0, may hold values from -6 to 6
- grad_out: bfloat16 [32768, 8192], P(('dp', 'ctx'), 'head'), parts along dimension 0, may hold values from -6 to 6
- vis_blocks: int32 [256, 6], P('dp'), parts along dimension 0, may hold values from 0 to 63, as said below
- vis_count: int32 [256], P('dp'), parts along dimension 0, may hold values from 1 to 6
- vis_len: int32 [256, 6], P('dp'), parts along dimension 0, may hold values from 1 to 128, as said below
Outputs:
- attention: bfloat16 [32768, 8192], P(('dp', 'ctx'), 'head'), parts along dimension 0
- grad_query: bfloat16 [32768, 8192], P(('dp', 'ctx'), 'head'), parts along dimension 0
- grad_key: bfloat16 [32768, 1024], P(('dp', 'ctx'), 'head'), parts along dimension 0
- grad_value: bfloat16 [32768, 1024], P(('dp', 'ctx'), 'head'), parts along dimension 0
There are 4 independent parts, one for each index of `dp`. A program takes and returns all parts, laid end to end along the dimension named above; each array names one. Nothing has to cross between parts.
Inputs may be any that keep to these rules, and one draw needn't show every extreme that they name: `vis_blocks`: slot 0 of row b is b itself; live slots 1 to vis_count[b] - 1 hold distinct blocks before b; slots at or past vis_count[b] hold b. Over the live slots of the 4 rows of one group of 4 consecutive query blocks, at most 2 distinct blocks of any other such group appear. `vis_len`: slot 0 and slots at or past vis_count hold 128.
All inputs are finite; a program needn't handle non-finite values.
Results may differ from a plain program's by a relative error of at most 0.012.
Values may be sent and summed in bfloat16 or wider, within the bound.
A program may use at most 128 MiB of HBM per device.

v0:
```python
import math

import jax
import jax.numpy as jnp
from jax import lax
from jax.sharding import PartitionSpec as P

HEAD_SIZE = 128
MASK_BLOCK_SIZE = 128


masked_score = -1e30


def attend(
    query_block_rows,
    gradient_block_rows,
    key_value_slots,
    block_id,
    row_blocks,
    row_count,
    row_lens,
):
    block_rows = query_block_rows.shape[0]
    total_slot_count = key_value_slots.shape[0]
    key_value_width = key_value_slots.shape[2] // 2
    kv_heads = key_value_width // HEAD_SIZE
    group_width_count = query_block_rows.shape[1] // key_value_width
    inv_root = 1.0 / math.sqrt(HEAD_SIZE)
    query_rows = query_block_rows.reshape(block_rows, kv_heads, group_width_count, HEAD_SIZE)
    output_gradients = gradient_block_rows.reshape(
        block_rows, kv_heads, group_width_count, HEAD_SIZE
    )
    key_portion = key_value_slots[:, :, :key_value_width].reshape(
        total_slot_count, block_rows, kv_heads, HEAD_SIZE
    )
    value_portion = key_value_slots[:, :, key_value_width:].reshape(
        total_slot_count, block_rows, kv_heads, HEAD_SIZE
    )
    query_pos = jnp.arange(block_rows, dtype=jnp.int32)[:, None, None]
    key_pos = jnp.arange(block_rows, dtype=jnp.int32)[None, None, :]
    slot_pos = jnp.arange(total_slot_count, dtype=jnp.int32)[None, :, None]
    visible = (slot_pos < row_count) & (key_pos < row_lens[None, :, None])
    visible = visible & ((row_blocks[None, :, None] != block_id) | (key_pos <= query_pos))
    scores = (
        jnp.einsum("qgrd,vkgd->grqvk", query_rows, key_portion, preferred_element_type=jnp.float32)
        * inv_root
    )
    row_max = jnp.max(jnp.where(visible, scores, masked_score), axis=(3, 4), keepdims=True)
    weights = jnp.exp(jnp.where(visible, scores - row_max, masked_score))
    soft_probs = weights / jnp.sum(weights, axis=(3, 4), keepdims=True)
    probs_low = soft_probs.astype(jnp.bfloat16)
    attention = jnp.einsum(
        "grqvk,vkgd->qgrd", probs_low, value_portion, preferred_element_type=jnp.float32
    )
    attention = attention.astype(jnp.bfloat16).reshape(block_rows, -1)
    dprobs = jnp.einsum(
        "qgrd,vkgd->grqvk", output_gradients, value_portion, preferred_element_type=jnp.float32
    )
    row_delta = jnp.sum(soft_probs * dprobs, axis=(3, 4), keepdims=True)
    dscores = (soft_probs * (dprobs - row_delta) * inv_root).astype(jnp.bfloat16)
    grad_query = jnp.einsum(
        "grqvk,vkgd->qgrd", dscores, key_portion, preferred_element_type=jnp.float32
    )
    grad_query = grad_query.astype(jnp.bfloat16).reshape(block_rows, -1)
    grad_keys = jnp.einsum(
        "grqvk,qgrd->vkgd", dscores, query_rows, preferred_element_type=jnp.float32
    )
    grad_values = jnp.einsum(
        "grqvk,qgrd->vkgd", probs_low, output_gradients, preferred_element_type=jnp.float32
    )
    grad_keys = grad_keys.reshape(total_slot_count, block_rows, key_value_width)
    grad_values = grad_values.reshape(total_slot_count, block_rows, key_value_width)
    return (attention, grad_query, jnp.concatenate([grad_keys, grad_values], axis=2))


def body(query_states, key_states, value_state_rows, grad_out, vis_blocks, vis_count, vis_len):
    shard_tokens = query_states.shape[0]
    per_shard = shard_tokens // MASK_BLOCK_SIZE
    total_blocks = vis_blocks.shape[0]
    total_slot_count = vis_blocks.shape[1]
    my_index = lax.axis_index("ctx")
    local_kv = jnp.concatenate([key_states, value_state_rows], axis=1)
    kv_total = local_kv.shape[1]
    key_value_width = key_states.shape[1]
    first_block = my_index * per_shard
    my_blocks = lax.dynamic_slice_in_dim(vis_blocks, first_block, per_shard, 0)
    my_count = lax.dynamic_slice_in_dim(vis_count, first_block, per_shard, 0)
    my_lens = lax.dynamic_slice_in_dim(vis_len, first_block, per_shard, 0)
    block_ids = first_block + jnp.arange(per_shard, dtype=jnp.int32)
    gathered = lax.all_gather(local_kv, "ctx", axis=0, tiled=True)
    all_blocks = gathered.reshape(total_blocks, MASK_BLOCK_SIZE, kv_total)
    key_value_slots = all_blocks[my_blocks]

    def one_block(pieces):
        (
            query_block_rows,
            gradient_block_rows,
            slot_block,
            block_id,
            row_blocks,
            row_count,
            row_lens,
        ) = pieces
        return attend(
            query_block_rows,
            gradient_block_rows,
            slot_block,
            block_id,
            row_blocks,
            row_count,
            row_lens,
        )

    attention, grad_query, slot_grads = lax.map(
        one_block,
        (
            query_states.reshape(per_shard, MASK_BLOCK_SIZE, -1),
            grad_out.reshape(per_shard, MASK_BLOCK_SIZE, -1),
            key_value_slots,
            block_ids,
            my_blocks,
            my_count,
            my_lens,
        ),
    )
    flat_grads = slot_grads.reshape(per_shard * total_slot_count, MASK_BLOCK_SIZE * kv_total)
    all_index = jnp.arange(total_blocks, dtype=jnp.int32)
    one_hot = (all_index[:, None] == my_blocks.reshape(-1)[None, :]).astype(jnp.float32)
    dense_part = jnp.dot(
        one_hot, flat_grads, precision=lax.Precision.HIGHEST, preferred_element_type=jnp.float32
    )
    summed = lax.psum_scatter(
        dense_part.reshape(total_blocks * MASK_BLOCK_SIZE, kv_total).astype(jnp.bfloat16),
        "ctx",
        scatter_dimension=0,
        tiled=True,
    ).astype(jnp.float32)
    grad_key = summed[:, :key_value_width].astype(jnp.bfloat16)
    grad_value = summed[:, key_value_width:].astype(jnp.bfloat16)
    return (
        attention.reshape(shard_tokens, -1),
        grad_query.reshape(shard_tokens, -1),
        grad_key,
        grad_value,
    )


def solution(mesh):
    in_specs = (
        P(("dp", "ctx"), "head"),
        P(("dp", "ctx"), "head"),
        P(("dp", "ctx"), "head"),
        P(("dp", "ctx"), "head"),
        P("dp", None),
        P("dp"),
        P("dp", None),
    )
    out_specs = (
        P(("dp", "ctx"), "head"),
        P(("dp", "ctx"), "head"),
        P(("dp", "ctx"), "head"),
        P(("dp", "ctx"), "head"),
    )
    return jax.shard_map(body, mesh=mesh, in_specs=in_specs, out_specs=out_specs, check_vma=False)
```

profile of v0, /device:TPU:36, one launch (start us, length us, event | category | flops | bytes accessed | tf_op | source)
XLA Modules:
  0.0 591.6 jit_solution(2314800535027185714)
XLA Ops:
  11.6 183.4 %all-gather.2.cloned.1.call-done = bf16[8192,512]{1,0:T(8,128)(2,1)} async-done(((bf16[512,512]{1,0:T(8,128)(2,1)}), bf16[8192,512]{1,0:T(8,128)(2,1)}) %all-gather.2.cloned.1.call-update) | async-done | bytes 8388624 | tf_op jit(solution)/shard_map/all_gather | solution.py:91
  194.9 6.0 %gather_fusion = bf16[24,128,512]{2,1,0:T(8,128)(2,1)} fusion(bf16[64,128,512]{2,1,0:T(8,128)(2,1)} %bitcast.187, s32[1024]{0:T(1024)S(1)} %pad_clamp_fusion), kind=kCustom, calls=%fused_computation | custom fusion | bytes 6291552 | tf_op jit(solution)/shard_map/gather | solution.py:93
  200.9 170.1 %while.14 = (s32[]{:T(128)}, bf16[4,128,2048]{2,1,0:T(8,128)(2,1)}, bf16[4,128,2048]{2,1,0:T(8,128)(2,1)}, f32[4,6,128,512]{3,2,1,0:T(8,128)}, bf16[4,6,128,512]...) while((s32[]{:T(128)}, bf16[4,128,2048]{2,1,0:T(8,128)(2,1)}, ...), condition=%wide.region_4.5_spmd, body=%wide.region_0.4_spmd.sunk | while | flops 2451648000 | bytes 174140432 | solution.py:115
  208.7 2.6 copy-done
  216.0 4.4 fusion.78
  220.4 2.6 fusion.79
  227.2 3.2 copy.152
  230.4 2.8 constant_dynamic-update-slice_fusion.6
  233.2 3.4 fusion.81
  251.3 2.6 copy-done
  258.5 4.4 fusion.78
  263.0 2.6 fusion.79
  269.8 3.2 copy.152
  273.0 2.8 constant_dynamic-update-slice_fusion.6
  275.7 3.4 fusion.81
  293.8 2.6 copy-done
  301.0 4.4 fusion.78
  305.5 2.6 fusion.79
  312.3 3.2 copy.152
  315.5 2.8 constant_dynamic-update-slice_fusion.6
  318.3 3.4 fusion.81
  326.4 2.1 constant_dynamic-update-slice_fusion.5
  336.3 2.6 copy-done
  343.6 4.4 fusion.78
  348.0 2.6 fusion.79
  354.8 3.2 copy.152
  358.0 2.8 constant_dynamic-update-slice_fusion.6
  360.8 3.4 fusion.81
  371.0 6.4 %copy.100 = f32[3,8,128,512]{3,1,2,0:T(8,128)S(1)} copy(f32[3,8,128,512]{3,2,1,0:T(8,128)} %bitcast.184) | data formatting | bytes 12582912
  377.5 8.9 %convolution_convert_fusion = bf16[64,65536]{1,0:T(8,128)(2,1)} fusion(f32[24,65536]{1,0:T(8,128)S(1)} %bitcast.178, s32[24]{0:T(128)S(1)} %copy-done.6), kind=kOutput, calls=%fused_computation.47 | convolution fusion | flops 1212155392 | bytes 14680160 | tf_op jit(solution)/shard_map/dot_general | solution.py:130
  386.3 10.6 %convert_element_type.29 = bf16[8192,512]{1,0:T(8,128)(2,1)} reshape(bf16[64,65536]{1,0:T(8,128)(2,1)} %convolution_convert_fusion) | data formatting | bytes 16777216 | tf_op jit(solution)/shard_map/convert_element_type | solution.py:134
  396.9 186.0 %reduce-scatter.2.cloned.1.call-done = bf16[512,512]{1,0:T(8,128)(2,1)} async-done(((bf16[8192,512]{1,0:T(8,128)(2,1)}), bf16[512,512]{1,0:T(8,128)(2,1)}) %reduce-scatter.2.cloned.1.call-update) | async-done | bytes 524304 | tf_op jit(solution)/shard_map/reduce_scatter | solution.py:133
  (187 shorter events, 97.6 us)
Async XLA Ops:
  7.2 187.8 %all-gather.2.cloned.1.call-start = ((), (), s32[]{:S(2)}) async-start(), calls=%async_computation.1 | async-start | bytes 8912896 | tf_op jit(solution)/shard_map/all_gather | solution.py:91
  9.1 573.8 %reduce-scatter.2.cloned.1.call-start = ((), (), s32[]{:S(2)}) async-start(), calls=%async_computation.2 | async-start | bytes 8912896 | tf_op jit(solution)/shard_map/reduce_scatter | solution.py:133
  206.1 6.5 %copy-start.4 = (bf16[6,128,256]{1,2,0:T(8,128)(2,1)}, bf16[6,128,256]{1,2,0:T(8,128)(2,1)S(1)}, u32[]{:S(2)}) copy-start(bf16[6,128,256]{1,2,0:T(8,128)(2,1)S(1)} %get-tuple-element.190) | copy-start | bytes 1179652 | tf_op jit(solution)/shard_map/while
  208.7 2.6 copy-start
  214.5 5.9 slice-start
  216.0 4.5 slice-start.1
  223.0 1.7 copy-start.1
  223.0 2.9 copy-start.3
  227.2 11.4 %copy-start.2 = (bf16[2,8,128,6,128]{2,4,1,3,0:T(8,128)(2,1)S(1)}, bf16[2,8,128,6,128]{2,4,1,3,0:T(8,128)(2,1)}, u32[]{:S(2)}) copy-start(bf16[2,8,128,6,128]{2,4,1,3,0:T(8,128)(2,1)} %copy-done.1) | copy-start | bytes 9437188 | tf_op jit(solution)/shard_map/while
  227.2 11.4 %copy-start.5 = (bf16[6,128,256]{1,2,0:T(8,128)(2,1)S(1)}, bf16[6,128,256]{1,2,0:T(8,128)(2,1)}, u32[]{:S(2)}) copy-start(bf16[6,128,256]{1,2,0:T(8,128)(2,1)} %copy-done.4) | copy-start | bytes 1179652 | tf_op jit(solution)/shard_map/while
  248.6 6.5 %copy-start.4 = (bf16[6,128,256]{1,2,0:T(8,128)(2,1)}, bf16[6,128,256]{1,2,0:T(8,128)(2,1)S(1)}, u32[]{:S(2)}) copy-start(bf16[6,128,256]{1,2,0:T(8,128)(2,1)S(1)} %get-tuple-element.190) | copy-start | bytes 1179652 | tf_op jit(solution)/shard_map/while
  251.3 2.6 copy-start
  257.0 5.9 slice-start
  258.5 4.5 slice-start.1
  265.6 2.9 copy-start.3
  269.8 11.4 %copy-start.2 = (bf16[2,8,128,6,128]{2,4,1,3,0:T(8,128)(2,1)S(1)}, bf16[2,8,128,6,128]{2,4,1,3,0:T(8,128)(2,1)}, u32[]{:S(2)}) copy-start(bf16[2,8,128,6,128]{2,4,1,3,0:T(8,128)(2,1)} %copy-done.1) | copy-start | bytes 9437188 | tf_op jit(solution)/shard_map/while
  269.8 11.4 %copy-start.5 = (bf16[6,128,256]{1,2,0:T(8,128)(2,1)S(1)}, bf16[6,128,256]{1,2,0:T(8,128)(2,1)}, u32[]{:S(2)}) copy-start(bf16[6,128,256]{1,2,0:T(8,128)(2,1)} %copy-done.4) | copy-start | bytes 1179652 | tf_op jit(solution)/shard_map/while
  291.2 6.5 %copy-start.4 = (bf16[6,128,256]{1,2,0:T(8,128)(2,1)}, bf16[6,128,256]{1,2,0:T(8,128)(2,1)S(1)}, u32[]{:S(2)}) copy-start(bf16[6,128,256]{1,2,0:T(8,128)(2,1)S(1)} %get-tuple-element.190) | copy-start | bytes 1179652 | tf_op jit(solution)/shard_map/while
  293.8 2.6 copy-start
  299.5 5.9 slice-start
  301.0 4.5 slice-start.1
  308.1 2.9 copy-start.3
  312.3 11.4 %copy-start.2 = (bf16[2,8,128,6,128]{2,4,1,3,0:T(8,128)(2,1)S(1)}, bf16[2,8,128,6,128]{2,4,1,3,0:T(8,128)(2,1)}, u32[]{:S(2)}) copy-start(bf16[2,8,128,6,128]{2,4,1,3,0:T(8,128)(2,1)} %copy-done.1) | copy-start | bytes 9437188 | tf_op jit(solution)/shard_map/while
  312.3 11.4 %copy-start.5 = (bf16[6,128,256]{1,2,0:T(8,128)(2,1)S(1)}, bf16[6,128,256]{1,2,0:T(8,128)(2,1)}, u32[]{:S(2)}) copy-start(bf16[6,128,256]{1,2,0:T(8,128)(2,1)} %copy-done.4) | copy-start | bytes 1179652 | tf_op jit(solution)/shard_map/while
  333.7 6.5 %copy-start.4 = (bf16[6,128,256]{1,2,0:T(8,128)(2,1)}, bf16[6,128,256]{1,2,0:T(8,128)(2,1)S(1)}, u32[]{:S(2)}) copy-start(bf16[6,128,256]{1,2,0:T(8,128)(2,1)S(1)} %get-tuple-element.190) | copy-start | bytes 1179652 | tf_op jit(solution)/shard_map/while
  336.3 2.6 copy-start
  342.1 5.9 slice-start
  343.5 4.5 slice-start.1
  350.6 2.9 copy-start.3
  354.8 11.4 %copy-start.2 = (bf16[2,8,128,6,128]{2,4,1,3,0:T(8,128)(2,1)S(1)}, bf16[2,8,128,6,128]{2,4,1,3,0:T(8,128)(2,1)}, u32[]{:S(2)}) copy-start(bf16[2,8,128,6,128]{2,4,1,3,0:T(8,128)(2,1)} %copy-done.1) | copy-start | bytes 9437188 | tf_op jit(solution)/shard_map/while
  354.8 11.4 %copy-start.5 = (bf16[6,128,256]{1,2,0:T(8,128)(2,1)S(1)}, bf16[6,128,256]{1,2,0:T(8,128)(2,1)}, u32[]{:S(2)}) copy-start(bf16[6,128,256]{1,2,0:T(8,128)(2,1)} %copy-done.4) | copy-start | bytes 1179652 | tf_op jit(solution)/shard_map/while
  371.0 6.4 %copy-start.6 = (s32[24]{0:T(128)S(1)}, s32[24]{0:T(128)}, u32[]{:S(2)}) copy-start(s32[24]{0:T(128)} %eq.16) | copy-start | bytes 292
  (3 other events, 5.2 us)
Sparse Core Ops, SparseCore 0:
  9.8 185.1 all-gather.1
  397.1 185.8 reduce-scatter.1
where the time goes:
time: 600 us; the launch traced here: 592 us
  waiting for transfers between devices  369 us (62%)
  local copies, waits for them, and re-layouts  119 us (20%)
  matrix products  59.4 us (10%)
  other arithmetic  28.5 us (5%)
  between operations  14.1 us (2%)
    reduce_scatter x1, waiting for transfers between devices, body(): lax.psum_scatter(dense_part.reshape(total_blocks * MASK_BLOCK_SIZE, kv_to...  186 us
    all_gather x1, waiting for transfers between devices, body(): gathered = lax.all_gather(local_kv, 'ctx', axis=0, tiled=True)  183 us
    dynamic_update_slice x20, local copies, waits for them, and re-layouts, body(): lax.map(one_block, (query_states.reshape(per_shard, MASK_BLOCK_SIZE, -1),...  45.4 us
    dynamic_slice x32, local copies, waits for them, and re-layouts, body(): lax.map(one_block, (query_states.reshape(per_shard, MASK_BLOCK_SIZE, -1),...  30.6 us
    dot_general x4, matrix products, attend(): jnp.einsum('qgrd,vkgd->grqvk', output_gradients, value_portion, preferred...  17.7 us
    dot_general x4, matrix products, attend(): jnp.einsum('grqvk,vkgd->qgrd', probs_low, value_portion, preferred_elemen...  13.6 us
    while x64, local copies, waits for them, and re-layouts  12.5 us
  transfers between devices with their start and end apart: 2, of which 2 were waited for; matrix products, arithmetic and copies ran while one was open for 0% of the time, Pallas kernels for 0%

commit v1 on v0

v1 whole, which is shorter than its diff:
```python
import functools
import math

import jax
import jax.numpy as jnp
from jax import lax
from jax.experimental import pallas as pl
from jax.experimental.pallas import tpu as pltpu
from jax.sharding import PartitionSpec as P

D = 128
BLOCK = 128
PER = 4
CTX = 16
VIS = 6
CAP = 2
NEG = -1e30
INV_ROOT = 1.0 / math.sqrt(D)
EXP2_SCALE = INV_ROOT * math.log2(math.e)
MIB = 1 << 20


def barrier_all(me):
    barrier = pltpu.get_barrier_semaphore()
    for k in range(1, CTX):
        pl.semaphore_signal(
            barrier,
            inc=1,
            device_id={"ctx": lax.rem(me + k, CTX)},
            device_id_type=pl.DeviceIdType.MESH,
        )
    pl.semaphore_wait(barrier, CTX - 1)


def chosen(blocks_ref, count_ref, dst, src):
    low = jnp.int32(PER - 1)
    high = jnp.int32(0)
    for r in range(PER):
        row = dst * PER + r
        count = count_ref[row]
        for s in range(1, VIS):
            t = blocks_ref[row * VIS + s] - src * PER
            hit = (t >= 0) & (t < PER) & (s < count)
            low = jnp.minimum(low, jnp.where(hit, t, PER - 1))
            high = jnp.maximum(high, jnp.where(hit, t, 0))
    return low, high


def exchange_kernel(blocks_ref, count_ref, k_ref, v_ref, out_ref, packed, send_sem, recv_sem, own_sem):
    me = lax.axis_index("ctx")
    width = k_ref.shape[1]
    for t in range(PER):
        rows = pl.ds(t * BLOCK, BLOCK)
        packed[0, t, :, :width] = k_ref[rows, :]
        packed[0, t, :, width:] = v_ref[rows, :]
    own = pltpu.make_async_copy(packed.at[0], out_ref.at[pl.ds(0, PER)], own_sem)
    own.start()
    barrier_all(me)

    def copy_to(k):
        return pltpu.make_async_remote_copy(
            src_ref=packed.at[k, pl.ds(0, CAP)],
            dst_ref=out_ref.at[pl.ds(PER + CAP * me, CAP)],
            send_sem=send_sem.at[k],
            recv_sem=recv_sem.at[me],
            device_id={"ctx": me + k},
            device_id_type=pl.DeviceIdType.MESH,
        )

    def arrival(src):
        return pltpu.make_async_remote_copy(
            src_ref=packed.at[1, pl.ds(0, CAP)],
            dst_ref=out_ref.at[pl.ds(PER + CAP * src, CAP)],
            send_sem=send_sem.at[0],
            recv_sem=recv_sem.at[src],
            device_id={"ctx": me},
            device_id_type=pl.DeviceIdType.MESH,
        )

    @pl.loop(1, CTX - me)
    def _(k):
        for c, t in enumerate(chosen(blocks_ref, count_ref, me + k, me)):
            for ref, lanes in ((k_ref, pl.ds(0, width)), (v_ref, pl.ds(width, width))):
                block = ref[pl.ds(0, BLOCK), :]
                for other in range(1, PER):
                    block = jnp.where(t == other, ref[pl.ds(other * BLOCK, BLOCK), :], block)
                packed[k, c, :, lanes] = block
        copy_to(k).start()

    @pl.loop(0, me)
    def _(src):
        arrival(src).wait_recv()

    @pl.loop(1, CTX - me)
    def _(k):
        copy_to(k).wait_send()

    own.wait()


def attend_kernel(
    blocks_ref, count_ref, len_ref, q_ref, do_ref, kv_ref, attn_ref, dq_ref, part_ref,
    qs, dos, scores, dprobs, acc, place, low,
):
    i, g = pl.program_id(0), pl.program_id(1)
    me = lax.axis_index("ctx")
    heads = q_ref.shape[1] // D
    lanes = heads * BLOCK
    row = me * PER + i
    count = count_ref[row]

    @pl.when((i == 0) & (g == 0))
    def _():
        acc[...] = jnp.zeros_like(acc)
        for src in range(CTX):
            low[src] = PER
        for r in range(PER):
            for s in range(1, VIS):
                block = blocks_ref[(me * PER + r) * VIS + s]
                src = block // PER
                live = s < count_ref[me * PER + r]
                low[src] = jnp.where(live, jnp.minimum(low[src], block - src * PER), low[src])
        for r in range(PER):
            place[r * VIS] = r
            for s in range(1, VIS):
                block = blocks_ref[(me * PER + r) * VIS + s]
                src = block // PER
                t = block - src * PER
                far = PER + CAP * src + jnp.where(t == low[src], 0, 1)
                place[r * VIS + s] = jnp.where(src == me, t, far)

    for h in range(heads):
        qs[pl.ds(h * BLOCK, BLOCK), :] = q_ref[:, h * D : (h + 1) * D]
        dos[pl.ds(h * BLOCK, BLOCK), :] = do_ref[:, h * D : (h + 1) * D]

    k_at = pl.multiple_of(g * D, D)
    v_at = pl.multiple_of(kv_ref.shape[2] // 2 + g * D, D)
    nt = (((1,), (1,)), ((), ()))
    tn = (((0,), (0,)), ((), ()))
    f32 = jnp.float32
    key_pos = lax.broadcasted_iota(jnp.int32, (BLOCK, lanes), 0)

    def score(s, visible):
        at = place[i * VIS + s]
        raw = lax.dot_general(kv_ref[at, :, pl.ds(k_at, D)], qs[...], nt, preferred_element_type=f32)
        raw = jnp.where(visible, raw, NEG)
        scores[s] = raw
        return jnp.max(raw, axis=0, keepdims=True)

    query_pos = lax.rem(lax.broadcasted_iota(jnp.int32, (BLOCK, lanes), 1), BLOCK)
    top = score(0, key_pos <= query_pos)
    top = lax.fori_loop(
        1, count, lambda s, m: jnp.maximum(m, score(s, key_pos < len_ref[row * VIS + s])), top
    )
    shift = top * EXP2_SCALE

    def weigh(s, total):
        w = jnp.exp2(scores[s] * EXP2_SCALE - shift)
        scores[s] = w
        return total + jnp.sum(w, axis=0, keepdims=True)

    total = lax.fori_loop(0, count, weigh, jnp.zeros((1, lanes), f32))
    scale = 1.0 / total

    def mix(s, out):
        at = place[i * VIS + s]
        p = scores[s] * scale
        scores[s] = p
        low_p = p.astype(jnp.bfloat16)
        v = kv_ref[at, :, pl.ds(v_at, D)]
        acc[at, :, pl.ds(v_at, D)] += jnp.dot(low_p, dos[...], preferred_element_type=f32)
        dp = lax.dot_general(v, dos[...], nt, preferred_element_type=f32)
        dprobs[s] = dp
        attn, delta = out
        attn = attn + lax.dot_general(v, low_p, tn, preferred_element_type=f32)
        return attn, delta + jnp.sum(p * dp, axis=0, keepdims=True)

    attn, delta = lax.fori_loop(0, count, mix, (jnp.zeros((D, lanes), f32), jnp.zeros((1, lanes), f32)))
    for h in range(heads):
        attn_ref[:, h * D : (h + 1) * D] = attn[:, h * BLOCK : (h + 1) * BLOCK].T.astype(attn_ref.dtype)

    def back(s, dq):
        at = place[i * VIS + s]
        ds = (scores[s] * (dprobs[s] - delta) * INV_ROOT).astype(jnp.bfloat16)
        k = kv_ref[at, :, pl.ds(k_at, D)]
        acc[at, :, pl.ds(k_at, D)] += jnp.dot(ds, qs[...], preferred_element_type=f32)
        return dq + lax.dot_general(k, ds, tn, preferred_element_type=f32)

    dq = lax.fori_loop(0, count, back, jnp.zeros((D, lanes), f32))
    for h in range(heads):
        dq_ref[:, h * D : (h + 1) * D] = dq[:, h * BLOCK : (h + 1) * BLOCK].T.astype(dq_ref.dtype)

    @pl.when((i == pl.num_programs(0) - 1) & (g == pl.num_programs(1) - 1))
    def _():
        @pl.loop(0, acc.shape[0])
        def _(at):
            part_ref[at] = acc[at].astype(part_ref.dtype)


def return_kernel(blocks_ref, count_ref, part_ref, gk_ref, gv_ref, own, landed, total, send_sem, recv_sem, own_sem):
    me = lax.axis_index("ctx")
    width = gk_ref.shape[1]
    mine = pltpu.make_async_copy(part_ref.at[pl.ds(0, PER)], own, own_sem)
    mine.start()
    barrier_all(me)

    def copy_to(src):
        return pltpu.make_async_remote_copy(
            src_ref=part_ref.at[pl.ds(PER + CAP * src, CAP)],
            dst_ref=landed.at[me],
            send_sem=send_sem.at[src],
            recv_sem=recv_sem.at[me],
            device_id={"ctx": src},
            device_id_type=pl.DeviceIdType.MESH,
        )

    def arrival(dst):
        return pltpu.make_async_remote_copy(
            src_ref=part_ref.at[pl.ds(PER, CAP)],
            dst_ref=landed.at[dst],
            send_sem=send_sem.at[0],
            recv_sem=recv_sem.at[dst],
            device_id={"ctx": me},
            device_id_type=pl.DeviceIdType.MESH,
        )

    @pl.loop(0, me)
    def _(k):
        copy_to(me - 1 - k).start()

    mine.wait()
    total[...] = own[...].astype(jnp.float32)

    @pl.loop(me + 1, CTX)
    def _(dst):
        picks = chosen(blocks_ref, count_ref, dst, me)
        arrival(dst).wait_recv()
        for c in range(CAP):
            for t in range(PER):
                got = landed[dst, c].astype(jnp.float32)
                total[t] += jnp.where(picks[c] == t, got, 0.0)

    @pl.loop(0, me)
    def _(src):
        copy_to(src).wait_send()

    for t in range(PER):
        rows = pl.ds(t * BLOCK, BLOCK)
        gk_ref[rows, :] = total[t, :, :width].astype(gk_ref.dtype)
        gv_ref[rows, :] = total[t, :, width:].astype(gv_ref.dtype)


def body(query_states, key_states, value_state_rows, grad_out, vis_blocks, vis_count, vis_len):
    tokens, q_width = query_states.shape
    width = key_states.shape[1]
    kv_heads = width // D
    bf16, f32 = jnp.bfloat16, jnp.float32
    blocks = vis_blocks.reshape(-1)
    lens = vis_len.reshape(-1)
    held = PER + CAP * CTX
    smem = pl.BlockSpec(memory_space=pltpu.SMEM)
    vmem = pl.BlockSpec(memory_space=pltpu.VMEM)
    hbm = pl.BlockSpec(memory_space=pl.ANY)

    kv_all = pl.pallas_call(
        exchange_kernel,
        out_shape=jax.ShapeDtypeStruct((held, BLOCK, 2 * width), bf16),
        in_specs=[smem, smem, vmem, vmem],
        out_specs=hbm,
        scratch_shapes=[
            pltpu.VMEM((CTX, PER, BLOCK, 2 * width), bf16),
            pltpu.SemaphoreType.DMA((CTX,)),
            pltpu.SemaphoreType.DMA((CTX,)),
            pltpu.SemaphoreType.DMA,
        ],
        compiler_params=pltpu.CompilerParams(
            collective_id=0, has_side_effects=True, vmem_limit_bytes=24 * MIB
        ),
    )(blocks, vis_count, key_states, value_state_rows)

    heads_block = q_width // kv_heads
    lanes = heads_block // D * BLOCK
    tile = pl.BlockSpec((BLOCK, heads_block), lambda i, g: (i, g))
    attention, grad_query, part = pl.pallas_call(
        attend_kernel,
        grid=(PER, kv_heads),
        out_shape=(
            jax.ShapeDtypeStruct((tokens, q_width), bf16),
            jax.ShapeDtypeStruct((tokens, q_width), bf16),
            jax.ShapeDtypeStruct((held, BLOCK, 2 * width), bf16),
        ),
        in_specs=[smem, smem, smem, tile, tile, vmem],
        out_specs=(tile, tile, vmem),
        scratch_shapes=[
            pltpu.VMEM((lanes, D), bf16),
            pltpu.VMEM((lanes, D), bf16),
            pltpu.VMEM((VIS, BLOCK, lanes), f32),
            pltpu.VMEM((VIS, BLOCK, lanes), f32),
            pltpu.VMEM((held, BLOCK, 2 * width), f32),
            pltpu.SMEM((PER * VIS,), jnp.int32),
            pltpu.SMEM((CTX,), jnp.int32),
        ],
        compiler_params=pltpu.CompilerParams(vmem_limit_bytes=56 * MIB),
    )(blocks, vis_count, lens, query_states, grad_out, kv_all)

    grad_key, grad_value = pl.pallas_call(
        return_kernel,
        out_shape=(
            jax.ShapeDtypeStruct((tokens, width), bf16),
            jax.ShapeDtypeStruct((tokens, width), bf16),
        ),
        in_specs=[smem, smem, hbm],
        out_specs=(vmem, vmem),
        scratch_shapes=[
            pltpu.VMEM((PER, BLOCK, 2 * width), bf16),
            pltpu.VMEM((CTX, CAP, BLOCK, 2 * width), bf16),
            pltpu.VMEM((PER, BLOCK, 2 * width), f32),
            pltpu.SemaphoreType.DMA((CTX,)),
            pltpu.SemaphoreType.DMA((CTX,)),
            pltpu.SemaphoreType.DMA,
        ],
        compiler_params=pltpu.CompilerParams(
            collective_id=1, has_side_effects=True, vmem_limit_bytes=24 * MIB
        ),
    )(blocks, vis_count, part)
    return attention, grad_query, grad_key, grad_value


def solution(mesh):
    rows = P(("dp", "ctx"), "head")
    return jax.shard_map(
        body,
        mesh=mesh,
        in_specs=(rows, rows, rows, rows, P("dp", None), P("dp"), P("dp", None)),
        out_specs=(rows, rows, rows, rows),
        check_vma=False,
    )
```

time: 600 us -> 261 us (0.43)
  the two profiles are of different devices: /device:TPU:36 before, /device:TPU:135 now
where the time goes in v1:
time: 261 us; the launch traced here: 260 us
  Pallas kernels  248 us (95%)
  local copies, waits for them, and re-layouts  11.5 us (4%)
    pallas_call x1, Pallas kernels, body(): pl.pallas_call(return_kernel, out_shape=(jax.ShapeDtypeStruct((tokens, wi...  144 us
    pallas_call x1, Pallas kernels, body(): pl.pallas_call(exchange_kernel, out_shape=jax.ShapeDtypeStruct((held, BLO...  77.6 us
    pallas_call x1, Pallas kernels, body(): pl.pallas_call(attend_kernel, grid=(PER, kv_heads), out_shape=(jax.ShapeD...  26.3 us
    unnamed x20, local copies, waits for them, and re-layouts  10.7 us

profile of v1, /device:TPU:135, one launch (start us, length us, event | category | flops | bytes accessed | tf_op | source)
XLA Modules:
  0.0 260.4 jit_solution(6539335108751004680)
XLA Ops:
  0.6 0.8 copy.11
  1.4 0.1 reshape.14.blocks_ref
  1.5 0.0 copy-start.4
  1.6 0.8 copy.12
  2.3 0.7 reshape.15.len_ref
  3.1 0.0 copy-start.2
  3.1 0.9 copy-done.2
  4.0 0.0 copy-start.3
  4.0 0.9 copy-done.3
  5.0 0.0 copy-start.6
  5.0 0.7 copy-done.6
  5.6 77.6 %shard_map.102.kv_ref = bf16[36,128,512]{2,1,0:T(8,128)(2,1)S(1)} custom-call(s32[384]{0:T(512)S(1)} %reshape.14.blocks_ref, s32[64]{0:T(128)S(1)} %copy-done.6, bf16[512,256]{1,0:T(8,128)(2,1)S(1)} %copy-done.2, bf16[512,256]{1,0:T(8,128)(2,1)S(1)} %copy-done.3), custom_call_target="tpu_custom_call" | custom-call | tf_op jit(solution)/shard_map/pallas_call | solution.py:265
  83.2 0.0 copy-done.4
  83.2 0.0 copy-start
  83.3 2.1 copy-done
  85.4 0.0 copy-start.7
  85.4 26.3 %shard_map.103 = (bf16[512,2048]{1,0:T(8,128)(2,1)}, bf16[512,2048]{1,0:T(8,128)(2,1)}, bf16[36,128,512]{2,1,0:T(8,128)(2,1)}) custom-call(s32[384]{0:T(512)} %copy-done.4, s32[64]{0:T(128)} %count_ref.5, s32[384]{0:T(512)} %reshape.15.len_ref, bf16[512,2048]{1,0:T(8,128)(2,1)} %q_ref.1, bf16[512,2048]{1,0:T(8,128)(2,1)} %do_ref.1, bf16[36,128,512]{2,1,0:T(8,128)(2,1)} %copy-done), custom_call_target="tpu_custom_call" | custom-call | tf_op jit(solution)/shard_map/pallas_call | solution.py:284
  111.7 0.0 copy-done.7
  111.7 0.0 copy-start.1
  111.7 2.3 copy-done.1
  114.0 0.0 copy-start.5
  114.0 0.7 copy-done.5
  114.7 144.2 %shard_map.104 = (bf16[512,256]{1,0:T(8,128)(2,1)S(1)}, bf16[512,256]{1,0:T(8,128)(2,1)S(1)}) custom-call(s32[384]{0:T(512)S(1)} %copy-done.5, s32[64]{0:T(128)S(1)} %copy-done.7, bf16[36,128,512]{2,1,0:T(8,128)(2,1)S(1)} %copy-done.1), custom_call_target="tpu_custom_call" | custom-call | tf_op jit(solution)/shard_map/pallas_call | solution.py:306
  259.0 0.7 copy.15
  259.7 0.7 copy.16
Async XLA Ops:
  1.5 81.7 %copy-start.4 = (s32[384]{0:T(512)}, s32[384]{0:T(512)S(1)}, u32[]{:S(2)}) copy-start(s32[384]{0:T(512)S(1)} %reshape.14.blocks_ref) | copy-start | bytes 4612
  3.1 0.9 copy-start.2
  4.0 0.9 copy-start.3
  5.0 0.7 copy-start.6
  83.2 2.1 copy-start
  85.4 26.3 %copy-start.7 = (s32[64]{0:T(128)S(1)}, s32[64]{0:T(128)}, u32[]{:S(2)}) copy-start(s32[64]{0:T(128)} %count_ref.5) | copy-start | bytes 772
  111.7 2.3 copy-start.1
  114.0 0.7 copy-start.5

commit v2 on v1

--- a/solution.py
+++ b/solution.py
@@ -11,25 +11,38 @@
 D = 128
 BLOCK = 128
 PER = 4
-CTX = 16
+SIDE = 4
+CTX = SIDE * SIDE
 VIS = 6
 CAP = 2
+ROW = SIDE * PER
 NEG = -1e30
 INV_ROOT = 1.0 / math.sqrt(D)
 EXP2_SCALE = INV_ROOT * math.log2(math.e)
 MIB = 1 << 20
-
-
-def barrier_all(me):
+MESH = pl.DeviceIdType.MESH
+
+
+def coords():
+    me = lax.axis_index("ctx")
+    return me, me // SIDE, lax.rem(me, SIDE)
+
+
+def at(y, z):
+    return {"ctx": lax.rem(y + SIDE, SIDE) * SIDE + z}
+
+
+def barrier_neighbours(y, z):
     barrier = pltpu.get_barrier_semaphore()
-    for k in range(1, CTX):
-        pl.semaphore_signal(
-            barrier,
-            inc=1,
-            device_id={"ctx": lax.rem(me + k, CTX)},
-            device_id_type=pl.DeviceIdType.MESH,
-        )
-    pl.semaphore_wait(barrier, CTX - 1)
+
+    def greet(where):
+        pl.semaphore_signal(barrier, inc=1, device_id=where, device_id_type=MESH)
+
+    greet(at(y + 1, z))
+    greet(at(y - 1, z))
+    pl.when(z > 0)(lambda: greet(at(y, z - 1)))
+    pl.when(z < SIDE - 1)(lambda: greet(at(y, z + 1)))
+    pl.semaphore_wait(barrier, 2 + jnp.where(z > 0, 1, 0) + jnp.where(z < SIDE - 1, 1, 0))
 
 
 def chosen(blocks_ref, count_ref, dst, src):
@@ -46,56 +59,157 @@
     return low, high
 
 
-def exchange_kernel(blocks_ref, count_ref, k_ref, v_ref, out_ref, packed, send_sem, recv_sem, own_sem):
-    me = lax.axis_index("ctx")
+def far_at(y, z):
+    return pl.ds(ROW + (y * SIDE + z) * CAP, CAP)
+
+
+STEPS = 2 * SIDE - 1
+
+
+def nth(n, z):
+    d = (n + 1) // 2
+    return z + jnp.where(lax.rem(n, 2) == 1, -d, d), d
+
+
+def exchange_kernel(
+    blocks_ref, count_ref, k_ref, v_ref, out_ref,
+    row, packed, relay,
+    z_recv, up_send, down_send, far_recv, y_send, relay_recv, relay_send, keep_sem,
+):
+    me, y, z = coords()
     width = k_ref.shape[1]
     for t in range(PER):
         rows = pl.ds(t * BLOCK, BLOCK)
-        packed[0, t, :, :width] = k_ref[rows, :]
-        packed[0, t, :, width:] = v_ref[rows, :]
-    own = pltpu.make_async_copy(packed.at[0], out_ref.at[pl.ds(0, PER)], own_sem)
-    own.start()
-    barrier_all(me)
-
-    def copy_to(k):
-        return pltpu.make_async_remote_copy(
-            src_ref=packed.at[k, pl.ds(0, CAP)],
-            dst_ref=out_ref.at[pl.ds(PER + CAP * me, CAP)],
-            send_sem=send_sem.at[k],
-            recv_sem=recv_sem.at[me],
-            device_id={"ctx": me + k},
-            device_id_type=pl.DeviceIdType.MESH,
-        )
-
-    def arrival(src):
-        return pltpu.make_async_remote_copy(
-            src_ref=packed.at[1, pl.ds(0, CAP)],
-            dst_ref=out_ref.at[pl.ds(PER + CAP * src, CAP)],
-            send_sem=send_sem.at[0],
-            recv_sem=recv_sem.at[src],
-            device_id={"ctx": me},
-            device_id_type=pl.DeviceIdType.MESH,
-        )
-
-    @pl.loop(1, CTX - me)
-    def _(k):
-        for c, t in enumerate(chosen(blocks_ref, count_ref, me + k, me)):
-            for ref, lanes in ((k_ref, pl.ds(0, width)), (v_ref, pl.ds(width, width))):
-                block = ref[pl.ds(0, BLOCK), :]
-                for other in range(1, PER):
-                    block = jnp.where(t == other, ref[pl.ds(other * BLOCK, BLOCK), :], block)
-                packed[k, c, :, lanes] = block
-        copy_to(k).start()
-
-    @pl.loop(0, me)
-    def _(src):
-        arrival(src).wait_recv()
-
-    @pl.loop(1, CTX - me)
-    def _(k):
-        copy_to(k).wait_send()
-
-    own.wait()
+        row[z, t, :, :width] = k_ref[rows, :]
+        row[z, t, :, width:] = v_ref[rows, :]
+    barrier_neighbours(y, z)
+
+    def z_copy(zs, to, sems):
+        return pltpu.make_async_remote_copy(
+            src_ref=row.at[zs],
+            dst_ref=row.at[zs],
+            send_sem=sems.at[zs],
+            recv_sem=z_recv.at[zs],
+            device_id=at(y, to),
+            device_id_type=MESH,
+        )
+
+    def y_near(yd, zs):
+        return pltpu.make_async_remote_copy(
+            src_ref=packed.at[yd, zs],
+            dst_ref=out_ref.at[far_at(y, zs)],
+            send_sem=y_send.at[yd * SIDE + zs],
+            recv_sem=far_recv.at[y * SIDE + zs],
+            device_id=at(yd, z),
+            device_id_type=MESH,
+        )
+
+    def y_far(yd, zs):
+        return pltpu.make_async_remote_copy(
+            src_ref=packed.at[yd, zs],
+            dst_ref=relay.at[zs],
+            send_sem=y_send.at[yd * SIDE + zs],
+            recv_sem=relay_recv.at[zs],
+            device_id=at(jnp.where(y == 0, SIDE - 1, 2), z),
+            device_id_type=MESH,
+        )
+
+    def relay_copy(zs):
+        return pltpu.make_async_remote_copy(
+            src_ref=relay.at[zs],
+            dst_ref=out_ref.at[far_at(3 - y, zs)],
+            send_sem=relay_send.at[zs],
+            recv_sem=far_recv.at[(3 - y) * SIDE + zs],
+            device_id=at(5 - y, z),
+            device_id_type=MESH,
+        )
+
+    def keep(zs):
+        return pltpu.make_async_copy(row.at[zs], out_ref.at[pl.ds(zs * PER, PER)], keep_sem.at[zs])
+
+    def wanted(zs):
+        inside = (zs >= 0) & (zs < SIDE)
+        return inside, inside & ((zs <= z) | (y < SIDE - 1))
+
+    def pack(yd, zs):
+        picks = chosen(blocks_ref, count_ref, yd * SIDE + z, y * SIDE + zs)
+        for c in range(CAP):
+            block = row[zs, 0]
+            for t in range(1, PER):
+                block = jnp.where(picks[c] == t, row[zs, t], block)
+            packed[yd, zs, c] = block
+
+    def step(n):
+        zs, d = nth(n, z)
+        inside, mine = wanted(zs)
+
+        @pl.when(mine)
+        def _():
+            pl.when(d > 0)(lambda: z_copy(zs, z, up_send).wait_recv())
+            pl.when((zs <= z) & (z < SIDE - 1))(lambda: z_copy(zs, z + 1, up_send).start())
+            pl.when((zs >= z) & (z > 0) & (y < SIDE - 1))(
+                lambda: z_copy(zs, z - 1, down_send).start()
+            )
+            keep(zs).start()
+
+        @pl.when(inside)
+        def _():
+            @pl.loop(0, SIDE - 1 - y)
+            def _(h):
+                hop = jnp.where(y == 2, 1, jnp.where(h == 0, 2, jnp.where(h == 1, 1, 3)))
+                yd = y + hop
+                pack(yd, zs)
+                pl.when(hop == 2)(lambda: y_far(yd, zs).start())
+                pl.when(hop != 2)(lambda: y_near(yd, zs).start())
+
+    def relay_step(n):
+        zs, _ = nth(n, z)
+
+        @pl.when((zs >= 0) & (zs < SIDE) & (y >= 2))
+        def _():
+            pltpu.make_async_remote_copy(
+                src_ref=relay.at[zs],
+                dst_ref=relay.at[zs],
+                send_sem=relay_send.at[zs],
+                recv_sem=relay_recv.at[zs],
+                device_id=at(y, z),
+                device_id_type=MESH,
+            ).wait_recv()
+            relay_copy(zs).start()
+
+    @pl.loop(0, STEPS + 1)
+    def _(n):
+        pl.when(n < STEPS)(lambda: step(n))
+        pl.when(n > 0)(lambda: relay_step(n - 1))
+
+    @pl.loop(0, y * SIDE)
+    def _(n):
+        pltpu.make_async_remote_copy(
+            src_ref=packed.at[0, 0],
+            dst_ref=out_ref.at[pl.ds(ROW + n * CAP, CAP)],
+            send_sem=relay_send.at[0],
+            recv_sem=far_recv.at[n],
+            device_id=at(y, z),
+            device_id_type=MESH,
+        ).wait_recv()
+
+    @pl.loop(0, SIDE)
+    def _(zs):
+        _, mine = wanted(zs)
+
+        @pl.when(mine)
+        def _():
+            pl.when((zs <= z) & (z < SIDE - 1))(lambda: z_copy(zs, z + 1, up_send).wait_send())
+            pl.when((zs >= z) & (z > 0) & (y < SIDE - 1))(
+                lambda: z_copy(zs, z - 1, down_send).wait_send()
+            )
+            keep(zs).wait()
+
+        @pl.loop(y + 1, SIDE)
+        def _(yd):
+            y_near(yd, zs).wait_send()
+
+        pl.when(y >= 2)(lambda: relay_copy(zs).wait_send())
 
 
 def attend_kernel(
@@ -121,13 +235,14 @@
                 live = s < count_ref[me * PER + r]
                 low[src] = jnp.where(live, jnp.minimum(low[src], block - src * PER), low[src])
         for r in range(PER):
-            place[r * VIS] = r
+            place[r * VIS] = lax.rem(me, SIDE) * PER + r
             for s in range(1, VIS):
                 block = blocks_ref[(me * PER + r) * VIS + s]
                 src = block // PER
                 t = block - src * PER
-                far = PER + CAP * src + jnp.where(t == low[src], 0, 1)
-                place[r * VIS + s] = jnp.where(src == me, t, far)
+                far = ROW + CAP * src + jnp.where(t == low[src], 0, 1)
+                near = lax.rem(src, SIDE) * PER + t
+                place[r * VIS + s] = jnp.where(src // SIDE == me // SIDE, near, far)
 
     for h in range(heads):
         qs[pl.ds(h * BLOCK, BLOCK), :] = q_ref[:, h * D : (h + 1) * D]
@@ -197,57 +312,156 @@
             part_ref[at] = acc[at].astype(part_ref.dtype)
 
 
-def return_kernel(blocks_ref, count_ref, part_ref, gk_ref, gv_ref, own, landed, total, send_sem, recv_sem, own_sem):
-    me = lax.axis_index("ctx")
+def return_kernel(
+    blocks_ref, count_ref, part_ref, gk_ref, gv_ref,
+    own, landed, relay, running, from_left, from_right, total,
+    y_send, y_recv, relay_send, relay_recv, z_send, left_recv, right_recv, own_sem,
+):
+    me, y, z = coords()
     width = gk_ref.shape[1]
-    mine = pltpu.make_async_copy(part_ref.at[pl.ds(0, PER)], own, own_sem)
-    mine.start()
-    barrier_all(me)
-
-    def copy_to(src):
-        return pltpu.make_async_remote_copy(
-            src_ref=part_ref.at[pl.ds(PER + CAP * src, CAP)],
-            dst_ref=landed.at[me],
-            send_sem=send_sem.at[src],
-            recv_sem=recv_sem.at[me],
-            device_id={"ctx": src},
-            device_id_type=pl.DeviceIdType.MESH,
-        )
-
-    def arrival(dst):
-        return pltpu.make_async_remote_copy(
-            src_ref=part_ref.at[pl.ds(PER, CAP)],
-            dst_ref=landed.at[dst],
-            send_sem=send_sem.at[0],
-            recv_sem=recv_sem.at[dst],
-            device_id={"ctx": me},
-            device_id_type=pl.DeviceIdType.MESH,
-        )
-
-    @pl.loop(0, me)
-    def _(k):
-        copy_to(me - 1 - k).start()
-
-    mine.wait()
-    total[...] = own[...].astype(jnp.float32)
-
-    @pl.loop(me + 1, CTX)
-    def _(dst):
-        picks = chosen(blocks_ref, count_ref, dst, me)
-        arrival(dst).wait_recv()
-        for c in range(CAP):
-            for t in range(PER):
-                got = landed[dst, c].astype(jnp.float32)
-                total[t] += jnp.where(picks[c] == t, got, 0.0)
-
-    @pl.loop(0, me)
-    def _(src):
-        copy_to(src).wait_send()
+
+    def own_copy(zs):
+        return pltpu.make_async_copy(part_ref.at[pl.ds(zs * PER, PER)], own.at[zs], own_sem.at[zs])
+
+    for zs in range(SIDE):
+        pl.when(zs <= z)(lambda: own_copy(zs).start())
+    barrier_neighbours(y, z)
+
+    def y_near(ys, zs):
+        return pltpu.make_async_remote_copy(
+            src_ref=part_ref.at[far_at(ys, zs)],
+            dst_ref=landed.at[y, zs],
+            send_sem=y_send.at[ys * SIDE + zs],
+            recv_sem=y_recv.at[y * SIDE + zs],
+            device_id=at(ys, z),
+            device_id_type=MESH,
+        )
+
+    def y_far(ys, zs):
+        return pltpu.make_async_remote_copy(
+            src_ref=part_ref.at[far_at(ys, zs)],
+            dst_ref=relay.at[zs],
+            send_sem=y_send.at[ys * SIDE + zs],
+            recv_sem=relay_recv.at[zs],
+            device_id=at(5 - y, z),
+            device_id_type=MESH,
+        )
+
+    def relay_copy(zs):
+        return pltpu.make_async_remote_copy(
+            src_ref=relay.at[zs],
+            dst_ref=landed.at[5 - y, zs],
+            send_sem=relay_send.at[zs],
+            recv_sem=y_recv.at[(5 - y) * SIDE + zs],
+            device_id=at(3 - y, z),
+            device_id_type=MESH,
+        )
+
+    def z_copy(zs, to, landing, sems):
+        return pltpu.make_async_remote_copy(
+            src_ref=running.at[zs],
+            dst_ref=landing.at[zs],
+            send_sem=z_send.at[zs],
+            recv_sem=sems.at[zs],
+            device_id=at(y, to),
+            device_id_type=MESH,
+        )
+
+    def inside(zs):
+        return (zs >= 0) & (zs < SIDE)
+
+    @pl.loop(0, STEPS)
+    def _(n):
+        zs, _ = nth(STEPS - 1 - n, z)
+
+        @pl.when(inside(zs))
+        def _():
+            pl.when(y >= 2)(lambda: y_far(y - 2, zs).start())
+            pl.when(y >= 1)(lambda: y_near(y - 1, zs).start())
+            pl.when(y >= 3)(lambda: y_near(y - 3, zs).start())
+
+    def relay_step(n):
+        zs, _ = nth(n, z)
+
+        @pl.when(inside(zs) & (y >= 2))
+        def _():
+            pltpu.make_async_remote_copy(
+                src_ref=relay.at[zs],
+                dst_ref=relay.at[zs],
+                send_sem=relay_send.at[zs],
+                recv_sem=relay_recv.at[zs],
+                device_id=at(y, z),
+                device_id_type=MESH,
+            ).wait_recv()
+            relay_copy(zs).start()
+
+    def step(n):
+        zs, d = nth(n, z)
+
+        @pl.when(inside(zs) & ((zs <= z) | (y < SIDE - 1)))
+        def _():
+            @pl.when(zs <= z)
+            def _():
+                own_copy(zs).wait()
+                total[...] = own[zs].astype(jnp.float32)
+
+            @pl.when(zs > z)
+            def _():
+                total[...] = jnp.zeros_like(total)
+
+            @pl.loop(y + 1, SIDE)
+            def _(yd):
+                picks = chosen(blocks_ref, count_ref, yd * SIDE + z, y * SIDE + zs)
+                pltpu.make_async_remote_copy(
+                    src_ref=landed.at[yd, zs],
+                    dst_ref=landed.at[yd, zs],
+                    send_sem=relay_send.at[0],
+                    recv_sem=y_recv.at[yd * SIDE + zs],
+                    device_id=at(y, z),
+                    device_id_type=MESH,
+                ).wait_recv()
+                for c in range(CAP):
+                    for t in range(PER):
+                        got = landed[yd, zs, c].astype(jnp.float32)
+                        total[t] += jnp.where(picks[c] == t, got, 0.0)
+
+            @pl.when((zs <= z) & (z < SIDE - 1))
+            def _():
+                z_copy(zs, z, from_right, right_recv).wait_recv()
+                total[...] += from_right[zs].astype(jnp.float32)
+
+            @pl.when((zs >= z) & (z > 0) & (y < SIDE - 1))
+            def _():
+                z_copy(zs, z, from_left, left_recv).wait_recv()
+                total[...] += from_left[zs].astype(jnp.float32)
+
+            @pl.when(d > 0)
+            def _():
+                running[zs] = total[...].astype(running.dtype)
+                pl.when(zs < z)(lambda: z_copy(zs, z - 1, from_right, right_recv).start())
+                pl.when(zs > z)(lambda: z_copy(zs, z + 1, from_left, left_recv).start())
+
+    @pl.loop(0, STEPS)
+    def _(n):
+        relay_step(STEPS - 1 - n)
+        step(STEPS - 1 - n)
 
     for t in range(PER):
         rows = pl.ds(t * BLOCK, BLOCK)
         gk_ref[rows, :] = total[t, :, :width].astype(gk_ref.dtype)
         gv_ref[rows, :] = total[t, :, width:].astype(gv_ref.dtype)
+
+    @pl.loop(0, SIDE)
+    def _(zs):
+        pl.when((zs < z) | ((zs > z) & (y < SIDE - 1)))(
+            lambda: z_copy(zs, z, from_right, right_recv).wait_send()
+        )
+
+        @pl.loop(0, y)
+        def _(ys):
+            y_near(ys, zs).wait_send()
+
+        pl.when(y >= 2)(lambda: relay_copy(zs).wait_send())
 
 
 def body(query_states, key_states, value_state_rows, grad_out, vis_blocks, vis_count, vis_len):
@@ -257,7 +471,8 @@
     bf16, f32 = jnp.bfloat16, jnp.float32
     blocks = vis_blocks.reshape(-1)
     lens = vis_len.reshape(-1)
-    held = PER + CAP * CTX
+    held = ROW + CAP * SIDE * (SIDE - 1)
+    sems = lambda n: pltpu.SemaphoreType.DMA((n,))
     smem = pl.BlockSpec(memory_space=pltpu.SMEM)
     vmem = pl.BlockSpec(memory_space=pltpu.VMEM)
     hbm = pl.BlockSpec(memory_space=pl.ANY)
@@ -268,10 +483,17 @@
         in_specs=[smem, smem, vmem, vmem],
         out_specs=hbm,
         scratch_shapes=[
-            pltpu.VMEM((CTX, PER, BLOCK, 2 * width), bf16),
-            pltpu.SemaphoreType.DMA((CTX,)),
-            pltpu.SemaphoreType.DMA((CTX,)),
-            pltpu.SemaphoreType.DMA,
+            pltpu.VMEM((SIDE, PER, BLOCK, 2 * width), bf16),
+            pltpu.VMEM((SIDE, SIDE, CAP, BLOCK, 2 * width), bf16),
+            pltpu.VMEM((SIDE, CAP, BLOCK, 2 * width), bf16),
+            sems(SIDE),
+            sems(SIDE),
+            sems(SIDE),
+            sems(CTX),
+            sems(CTX),
+            sems(SIDE),
+            sems(SIDE),
+            sems(SIDE),
         ],
         compiler_params=pltpu.CompilerParams(
             collective_id=0, has_side_effects=True, vmem_limit_bytes=24 * MIB
@@ -312,12 +534,21 @@
         in_specs=[smem, smem, hbm],
         out_specs=(vmem, vmem),
         scratch_shapes=[
-            pltpu.VMEM((PER, BLOCK, 2 * width), bf16),
-            pltpu.VMEM((CTX, CAP, BLOCK, 2 * width), bf16),
+            pltpu.VMEM((SIDE, PER, BLOCK, 2 * width), bf16),
+            pltpu.VMEM((SIDE, SIDE, CAP, BLOCK, 2 * width), bf16),
+            pltpu.VMEM((SIDE, CAP, BLOCK, 2 * width), bf16),
+            pltpu.VMEM((SIDE, PER, BLOCK, 2 * width), bf16),
+            pltpu.VMEM((SIDE, PER, BLOCK, 2 * width), bf16),
+            pltpu.VMEM((SIDE, PER, BLOCK, 2 * width), bf16),
             pltpu.VMEM((PER, BLOCK, 2 * width), f32),
-            pltpu.SemaphoreType.DMA((CTX,)),
-            pltpu.SemaphoreType.DMA((CTX,)),
-            pltpu.SemaphoreType.DMA,
+            sems(CTX),
+            sems(CTX),
+            sems(SIDE),
+            sems(SIDE),
+            sems(SIDE),
+            sems(SIDE),
+            sems(SIDE),
+            sems(SIDE),
         ],
         compiler_params=pltpu.CompilerParams(
             collective_id=1, has_side_effects=True, vmem_limit_bytes=24 * MIB

time: 261 us -> 187 us (0.72)
  Pallas kernels: 248 us -> 175 us
    pallas_call x1, Pallas kernels: 144 us -> 104 us  [body(): pl.pallas_call(return_kernel, out_shape=(jax.ShapeDtypeStruct((tokens, wi...]
    pallas_call x1, Pallas kernels: 77.6 us -> 48.4 us  [body(): pl.pallas_call(exchange_kernel, out_shape=jax.ShapeDtypeStruct((held, BLO...]
    pallas_call x1, Pallas kernels: 26.3 us -> 22.3 us  [body(): pl.pallas_call(attend_kernel, grid=(PER, kv_heads), out_shape=(jax.ShapeD...]
where the time goes in v2:
time: 187 us
  Pallas kernels  175 us (94%)
  local copies, waits for them, and re-layouts  11.8 us (6%)
    pallas_call x1, Pallas kernels, body(): pl.pallas_call(return_kernel, out_shape=(jax.ShapeDtypeStruct((tokens, wi...  104 us
    pallas_call x1, Pallas kernels, body(): pl.pallas_call(exchange_kernel, out_shape=jax.ShapeDtypeStruct((held, BLO...  48.4 us
    pallas_call x1, Pallas kernels, body(): pl.pallas_call(attend_kernel, grid=(PER, kv_heads), out_shape=(jax.ShapeD...  22.3 us
    unnamed x20, local copies, waits for them, and re-layouts  11 us

profile of v2, /device:TPU:135, one launch (start us, length us, event | category | flops | bytes accessed | tf_op | source)
XLA Modules:
  0.0 187.0 jit_solution(2075527516729898407)
XLA Ops:
  0.6 0.8 copy.11
  1.4 0.1 reshape.14.blocks_ref
  1.5 0.0 copy-start.4
  1.6 0.8 copy.12
  2.3 0.7 reshape.15.len_ref
  3.1 0.0 copy-start.2
  3.1 0.9 copy-done.2
  4.0 0.0 copy-start.3
  4.0 0.9 copy-done.3
  5.0 0.0 copy-start.6
  5.0 0.7 copy-done.6
  5.6 48.4 %shard_map.102.kv_ref = bf16[40,128,512]{2,1,0:T(8,128)(2,1)S(1)} custom-call(s32[384]{0:T(512)S(1)} %reshape.14.blocks_ref, s32[64]{0:T(128)S(1)} %copy-done.6, bf16[512,256]{1,0:T(8,128)(2,1)S(1)} %copy-done.2, bf16[512,256]{1,0:T(8,128)(2,1)S(1)} %copy-done.3), custom_call_target="tpu_custom_call" | custom-call | tf_op jit(solution)/shard_map/pallas_call | solution.py:480
  54.0 0.0 copy-done.4
  54.0 0.0 copy-start
  54.1 2.3 %copy-done = bf16[40,128,512]{2,1,0:T(8,128)(2,1)} copy-done((bf16[40,128,512]{2,1,0:T(8,128)(2,1)}, bf16[40,128,512]{2,1,0:T(8,128)(2,1)S(1)}, u32[]{:S(2)}) %copy-start) | copy-done | bytes 5242904
  56.3 0.0 copy-start.7
  56.3 22.3 %shard_map.103 = (bf16[512,2048]{1,0:T(8,128)(2,1)}, bf16[512,2048]{1,0:T(8,128)(2,1)}, bf16[40,128,512]{2,1,0:T(8,128)(2,1)}) custom-call(s32[384]{0:T(512)} %copy-done.4, s32[64]{0:T(128)} %count_ref.5, s32[384]{0:T(512)} %reshape.15.len_ref, bf16[512,2048]{1,0:T(8,128)(2,1)} %q_ref.1, bf16[512,2048]{1,0:T(8,128)(2,1)} %do_ref.1, bf16[40,128,512]{2,1,0:T(8,128)(2,1)} %copy-done), custom_call_target="tpu_custom_call" | custom-call | tf_op jit(solution)/shard_map/pallas_call | solution.py:506
  78.7 0.0 copy-done.7
  78.7 0.0 copy-start.1
  78.7 2.5 %copy-done.1 = bf16[40,128,512]{2,1,0:T(8,128)(2,1)S(1)} copy-done((bf16[40,128,512]{2,1,0:T(8,128)(2,1)S(1)}, bf16[40,128,512]{2,1,0:T(8,128)(2,1)}, u32[]{:S(2)}) %copy-start.1) | copy-done | bytes 5242904
  81.2 0.0 copy-start.5
  81.2 0.7 copy-done.5
  81.9 103.8 %shard_map.104 = (bf16[512,256]{1,0:T(8,128)(2,1)S(1)}, bf16[512,256]{1,0:T(8,128)(2,1)S(1)}) custom-call(s32[384]{0:T(512)S(1)} %copy-done.5, s32[64]{0:T(128)S(1)} %copy-done.7, bf16[40,128,512]{2,1,0:T(8,128)(2,1)S(1)} %copy-done.1), custom_call_target="tpu_custom_call" | custom-call | tf_op jit(solution)/shard_map/pallas_call | solution.py:528
  185.6 0.7 copy.15
  186.3 0.7 copy.16
Async XLA Ops:
  1.5 52.5 %copy-start.4 = (s32[384]{0:T(512)}, s32[384]{0:T(512)S(1)}, u32[]{:S(2)}) copy-start(s32[384]{0:T(512)S(1)} %reshape.14.blocks_ref) | copy-start | bytes 4612
  3.1 0.9 copy-start.2
  4.0 0.9 copy-start.3
  5.0 0.7 copy-start.6
  54.0 2.3 %copy-start = (bf16[40,128,512]{2,1,0:T(8,128)(2,1)}, bf16[40,128,512]{2,1,0:T(8,128)(2,1)S(1)}, u32[]{:S(2)}) copy-start(bf16[40,128,512]{2,1,0:T(8,128)(2,1)S(1)} %shard_map.102.kv_ref) | copy-start | bytes 15728644
  56.3 22.3 %copy-start.7 = (s32[64]{0:T(128)S(1)}, s32[64]{0:T(128)}, u32[]{:S(2)}) copy-start(s32[64]{0:T(128)} %count_ref.5) | copy-start | bytes 772
  78.7 2.5 %copy-start.1 = (bf16[40,128,512]{2,1,0:T(8,128)(2,1)S(1)}, bf16[40,128,512]{2,1,0:T(8,128)(2,1)}, u32[]{:S(2)}) copy-start(bf16[40,128,512]{2,1,0:T(8,128)(2,1)} %get-tuple-element.11.part_ref) | copy-start | bytes 15728644
  81.2 0.7 copy-start.5

commit v3 on v2

--- a/solution.py
+++ b/solution.py
@@ -20,6 +20,7 @@
 INV_ROOT = 1.0 / math.sqrt(D)
 EXP2_SCALE = INV_ROOT * math.log2(math.e)
 MIB = 1 << 20
+CHUNK = 1024
 MESH = pl.DeviceIdType.MESH
 
 
@@ -214,14 +215,16 @@
 
 def attend_kernel(
     blocks_ref, count_ref, len_ref, q_ref, do_ref, kv_ref, attn_ref, dq_ref, part_ref,
-    qs, dos, scores, dprobs, acc, place, low,
+    qs, dos, qt, dot, keys, values, scores, attn_t, dq_t, acc, place, seen, low,
 ):
     i, g = pl.program_id(0), pl.program_id(1)
     me = lax.axis_index("ctx")
     heads = q_ref.shape[1] // D
     lanes = heads * BLOCK
+    width = kv_ref.shape[2] // 2
     row = me * PER + i
-    count = count_ref[row]
+    pairs = (count_ref[row] + 1) // 2
+    f32, bf16 = jnp.float32, jnp.bfloat16
 
     @pl.when((i == 0) & (g == 0))
     def _():
@@ -235,81 +238,102 @@
                 live = s < count_ref[me * PER + r]
                 low[src] = jnp.where(live, jnp.minimum(low[src], block - src * PER), low[src])
         for r in range(PER):
-            place[r * VIS] = lax.rem(me, SIDE) * PER + r
+            own = lax.rem(me, SIDE) * PER + r
+            place[r * VIS] = own
+            seen[r * VIS] = BLOCK
             for s in range(1, VIS):
                 block = blocks_ref[(me * PER + r) * VIS + s]
+                live = s < count_ref[me * PER + r]
                 src = block // PER
                 t = block - src * PER
                 far = ROW + CAP * src + jnp.where(t == low[src], 0, 1)
                 near = lax.rem(src, SIDE) * PER + t
-                place[r * VIS + s] = jnp.where(src // SIDE == me // SIDE, near, far)
+                there = jnp.where(src // SIDE == me // SIDE, near, far)
+                place[r * VIS + s] = jnp.where(live, there, own)
+                seen[r * VIS + s] = jnp.where(live, len_ref[(me * PER + r) * VIS + s], 0)
 
     for h in range(heads):
-        qs[pl.ds(h * BLOCK, BLOCK), :] = q_ref[:, h * D : (h + 1) * D]
-        dos[pl.ds(h * BLOCK, BLOCK), :] = do_ref[:, h * D : (h + 1) * D]
+        q = q_ref[:, h * D : (h + 1) * D]
+        do = do_ref[:, h * D : (h + 1) * D]
+        qs[pl.ds(h * BLOCK, BLOCK), :] = q
+        dos[pl.ds(h * BLOCK, BLOCK), :] = do
+        qt[:, h * BLOCK : (h + 1) * BLOCK] = q.T
+        dot[:, h * BLOCK : (h + 1) * BLOCK] = do.T
 
     k_at = pl.multiple_of(g * D, D)
-    v_at = pl.multiple_of(kv_ref.shape[2] // 2 + g * D, D)
-    nt = (((1,), (1,)), ((), ()))
+    v_at = pl.multiple_of(width + g * D, D)
+    for s in range(VIS):
+        rows = pl.ds(s * BLOCK, BLOCK)
+        keys[rows, :] = kv_ref[place[i * VIS + s], :, pl.ds(k_at, D)]
+        values[rows, :] = kv_ref[place[i * VIS + s], :, pl.ds(v_at, D)]
+
     tn = (((0,), (0,)), ((), ()))
-    f32 = jnp.float32
-    key_pos = lax.broadcasted_iota(jnp.int32, (BLOCK, lanes), 0)
-
-    def score(s, visible):
-        at = place[i * VIS + s]
-        raw = lax.dot_general(kv_ref[at, :, pl.ds(k_at, D)], qs[...], nt, preferred_element_type=f32)
-        raw = jnp.where(visible, raw, NEG)
-        scores[s] = raw
-        return jnp.max(raw, axis=0, keepdims=True)
-
-    query_pos = lax.rem(lax.broadcasted_iota(jnp.int32, (BLOCK, lanes), 1), BLOCK)
-    top = score(0, key_pos <= query_pos)
-    top = lax.fori_loop(
-        1, count, lambda s, m: jnp.maximum(m, score(s, key_pos < len_ref[row * VIS + s])), top
-    )
-    shift = top * EXP2_SCALE
-
-    def weigh(s, total):
-        w = jnp.exp2(scores[s] * EXP2_SCALE - shift)
-        scores[s] = w
-        return total + jnp.sum(w, axis=0, keepdims=True)
-
-    total = lax.fori_loop(0, count, weigh, jnp.zeros((1, lanes), f32))
-    scale = 1.0 / total
-
-    def mix(s, out):
-        at = place[i * VIS + s]
-        p = scores[s] * scale
-        scores[s] = p
-        low_p = p.astype(jnp.bfloat16)
-        v = kv_ref[at, :, pl.ds(v_at, D)]
-        acc[at, :, pl.ds(v_at, D)] += jnp.dot(low_p, dos[...], preferred_element_type=f32)
-        dp = lax.dot_general(v, dos[...], nt, preferred_element_type=f32)
-        dprobs[s] = dp
-        attn, delta = out
-        attn = attn + lax.dot_general(v, low_p, tn, preferred_element_type=f32)
-        return attn, delta + jnp.sum(p * dp, axis=0, keepdims=True)
-
-    attn, delta = lax.fori_loop(0, count, mix, (jnp.zeros((D, lanes), f32), jnp.zeros((1, lanes), f32)))
-    for h in range(heads):
-        attn_ref[:, h * D : (h + 1) * D] = attn[:, h * BLOCK : (h + 1) * BLOCK].T.astype(attn_ref.dtype)
-
-    def back(s, dq):
-        at = place[i * VIS + s]
-        ds = (scores[s] * (dprobs[s] - delta) * INV_ROOT).astype(jnp.bfloat16)
-        k = kv_ref[at, :, pl.ds(k_at, D)]
-        acc[at, :, pl.ds(k_at, D)] += jnp.dot(ds, qs[...], preferred_element_type=f32)
-        return dq + lax.dot_general(k, ds, tn, preferred_element_type=f32)
-
-    dq = lax.fori_loop(0, count, back, jnp.zeros((D, lanes), f32))
-    for h in range(heads):
-        dq_ref[:, h * D : (h + 1) * D] = dq[:, h * BLOCK : (h + 1) * BLOCK].T.astype(dq_ref.dtype)
+    key_pos = lax.broadcasted_iota(jnp.int32, (BLOCK, CHUNK), 0)
+    query_pos = lax.rem(lax.broadcasted_iota(jnp.int32, (BLOCK, CHUNK), 1), BLOCK)
+
+    def pair_rows(p):
+        return pl.ds(pl.multiple_of(p * 2 * BLOCK, 2 * BLOCK), 2 * BLOCK)
+
+    def add_to(p, at_lane, product):
+        for half in range(2):
+            acc[place[i * VIS + 2 * p + half], :, pl.ds(at_lane, D)] += product[
+                half * BLOCK : (half + 1) * BLOCK
+            ]
+
+    @pl.loop(0, lanes // CHUNK)
+    def _(c):
+        at_c = pl.ds(pl.multiple_of(c * CHUNK, CHUNK), CHUNK)
+
+        def score(p, top):
+            raw = jnp.dot(keys[pair_rows(p), :], qt[:, at_c], preferred_element_type=f32)
+            first = key_pos < seen[i * VIS + 2 * p]
+            first = first & ((key_pos <= query_pos) | (p > 0))
+            second = key_pos < seen[i * VIS + 2 * p + 1]
+            raw = jnp.where(jnp.concatenate([first, second], axis=0), raw, NEG)
+            scores[pair_rows(p), :] = raw
+            return jnp.maximum(top, jnp.max(raw, axis=0, keepdims=True))
+
+        top = lax.fori_loop(0, pairs, score, jnp.full((1, CHUNK), NEG, f32))
+        shift = top * EXP2_SCALE
+
+        def weigh(p, total):
+            w = jnp.exp2(scores[pair_rows(p), :] * EXP2_SCALE - shift)
+            scores[pair_rows(p), :] = w
+            return total + jnp.sum(w, axis=0, keepdims=True)
+
+        scale = 1.0 / lax.fori_loop(0, pairs, weigh, jnp.zeros((1, CHUNK), f32))
+        attn_t[...] = jnp.zeros_like(attn_t)
+        dq_t[...] = jnp.zeros_like(dq_t)
+
+        @pl.loop(0, pairs)
+        def _(p):
+            probs = scores[pair_rows(p), :] * scale
+            scores[pair_rows(p), :] = probs
+            probs = probs.astype(bf16)
+            add_to(p, v_at, jnp.dot(probs, dos[at_c, :], preferred_element_type=f32))
+            attn_t[...] += lax.dot_general(values[pair_rows(p), :], probs, tn, preferred_element_type=f32)
+
+        delta = jnp.sum(attn_t[...] * dot[:, at_c].astype(f32), axis=0, keepdims=True)
+
+        @pl.loop(0, pairs)
+        def _(p):
+            dprobs = jnp.dot(values[pair_rows(p), :], dot[:, at_c], preferred_element_type=f32)
+            ds = (scores[pair_rows(p), :] * (dprobs - delta)).astype(bf16)
+            add_to(p, k_at, jnp.dot(ds, qs[at_c, :], preferred_element_type=f32))
+            dq_t[...] += lax.dot_general(keys[pair_rows(p), :], ds, tn, preferred_element_type=f32)
+
+        for h in range(CHUNK // BLOCK):
+            to = pl.ds(pl.multiple_of((c * (CHUNK // BLOCK) + h) * D, D), D)
+            part = slice(h * BLOCK, (h + 1) * BLOCK)
+            attn_ref[:, to] = attn_t[:, part].astype(bf16).T
+            dq_ref[:, to] = (dq_t[:, part] * INV_ROOT).astype(bf16).T
 
     @pl.when((i == pl.num_programs(0) - 1) & (g == pl.num_programs(1) - 1))
     def _():
         @pl.loop(0, acc.shape[0])
         def _(at):
-            part_ref[at] = acc[at].astype(part_ref.dtype)
+            part_ref[at, :, :width] = (acc[at, :, :width] * INV_ROOT).astype(bf16)
+            part_ref[at, :, width:] = acc[at, :, width:].astype(bf16)
 
 
 def return_kernel(
@@ -420,10 +444,10 @@
                     device_id=at(y, z),
                     device_id_type=MESH,
                 ).wait_recv()
-                for c in range(CAP):
-                    for t in range(PER):
-                        got = landed[yd, zs, c].astype(jnp.float32)
-                        total[t] += jnp.where(picks[c] == t, got, 0.0)
+                for t in range(PER):
+                    got = jnp.where(picks[1] == t, landed[yd, zs, 1], jnp.zeros_like(landed[yd, zs, 1]))
+                    got = jnp.where(picks[0] == t, landed[yd, zs, 0], got)
+                    total[t] += got.astype(jnp.float32)
 
             @pl.when((zs <= z) & (z < SIDE - 1))
             def _():
@@ -462,6 +486,46 @@
             y_near(ys, zs).wait_send()
 
         pl.when(y >= 2)(lambda: relay_copy(zs).wait_send())
+
+
+def attend(blocks, counts, lens, query_states, grad_out, kv_all):
+    tokens, q_width = query_states.shape
+    held, _, width = kv_all.shape
+    width //= 2
+    kv_heads = width // D
+    bf16, f32 = jnp.bfloat16, jnp.float32
+    smem = pl.BlockSpec(memory_space=pltpu.SMEM)
+    vmem = pl.BlockSpec(memory_space=pltpu.VMEM)
+    heads_block = q_width // kv_heads
+    lanes = heads_block // D * BLOCK
+    tile = pl.BlockSpec((BLOCK, heads_block), lambda i, g: (i, g))
+    return pl.pallas_call(
+        attend_kernel,
+        grid=(PER, kv_heads),
+        out_shape=(
+            jax.ShapeDtypeStruct((tokens, q_width), bf16),
+            jax.ShapeDtypeStruct((tokens, q_width), bf16),
+            jax.ShapeDtypeStruct((held, BLOCK, 2 * width), bf16),
+        ),
+        in_specs=[smem, smem, smem, tile, tile, vmem],
+        out_specs=(tile, tile, vmem),
+        scratch_shapes=[
+            pltpu.VMEM((lanes, D), bf16),
+            pltpu.VMEM((lanes, D), bf16),
+            pltpu.VMEM((D, lanes), bf16),
+            pltpu.VMEM((D, lanes), bf16),
+            pltpu.VMEM((VIS * BLOCK, D), bf16),
+            pltpu.VMEM((VIS * BLOCK, D), bf16),
+            pltpu.VMEM((VIS * BLOCK, CHUNK), f32),
+            pltpu.VMEM((D, CHUNK), f32),
+            pltpu.VMEM((D, CHUNK), f32),
+            pltpu.VMEM((held, BLOCK, 2 * width), f32),
+            pltpu.SMEM((PER * VIS,), jnp.int32),
+            pltpu.SMEM((PER * VIS,), jnp.int32),
+            pltpu.SMEM((CTX,), jnp.int32),
+        ],
+        compiler_params=pltpu.CompilerParams(vmem_limit_bytes=56 * MIB),
+    )(blocks, counts, lens, query_states, grad_out, kv_all)
 
 
 def body(query_states, key_states, value_state_rows, grad_out, vis_blocks, vis_count, vis_len):
@@ -500,31 +564,9 @@
         ),
     )(blocks, vis_count, key_states, value_state_rows)
 
-    heads_block = q_width // kv_heads
-    lanes = heads_block // D * BLOCK
-    tile = pl.BlockSpec((BLOCK, heads_block), lambda i, g: (i, g))
-    attention, grad_query, part = pl.pallas_call(
-        attend_kernel,
-        grid=(PER, kv_heads),
-        out_shape=(
-            jax.ShapeDtypeStruct((tokens, q_width), bf16),
-            jax.ShapeDtypeStruct((tokens, q_width), bf16),
-            jax.ShapeDtypeStruct((held, BLOCK, 2 * width), bf16),
-        ),
-        in_specs=[smem, smem, smem, tile, tile, vmem],
-        out_specs=(tile, tile, vmem),
-        scratch_shapes=[
-            pltpu.VMEM((lanes, D), bf16),
-            pltpu.VMEM((lanes, D), bf16),
-            pltpu.VMEM((VIS, BLOCK, lanes), f32),
-            pltpu.VMEM((VIS, BLOCK, lanes), f32),
-            pltpu.VMEM((held, BLOCK, 2 * width), f32),
-            pltpu.SMEM((PER * VIS,), jnp.int32),
-            pltpu.SMEM((CTX,), jnp.int32),
-        ],
-        compiler_params=pltpu.CompilerParams(vmem_limit_bytes=56 * MIB),
-    )(blocks, vis_count, lens, query_states, grad_out, kv_all)
-
+    attention, grad_query, part = attend(
+        blocks, vis_count, lens, query_states, grad_out, kv_all
+    )
     grad_key, grad_value = pl.pallas_call(
         return_kernel,
         out_shape=(

time: 187 us -> 177 us (0.947)
  the two profiles are of different devices: /device:TPU:135 before, /device:TPU:36 now
where the time goes in v3:
time: 177 us; the launch traced here: 175 us
  Pallas kernels  163 us (92%)
  local copies, waits for them, and re-layouts  11.8 us (7%)
    pallas_call x1, Pallas kernels, body(): pl.pallas_call(return_kernel, out_shape=(jax.ShapeDtypeStruct((tokens, wi...  84.9 us
    pallas_call x1, Pallas kernels, body(): pl.pallas_call(exchange_kernel, out_shape=jax.ShapeDtypeStruct((held, BLO...  49.2 us
    pallas_call x1, Pallas kernels, attend(): pl.pallas_call(attend_kernel, grid=(PER, kv_heads), out_shape=(jax.ShapeD...  28.6 us
    unnamed x20, local copies, waits for them, and re-layouts  11 us

profile of v3, /device:TPU:36, one launch (start us, length us, event | category | flops | bytes accessed | tf_op | source)
XLA Modules:
  0.0 175.2 jit_solution(534924983194923885)
XLA Ops:
  0.6 0.8 copy.11
  1.4 0.1 reshape.14.blocks_ref
  1.5 0.0 copy-start.4
  1.6 0.8 copy.12
  2.3 0.7 reshape.15.len_ref
  3.1 0.0 copy-start.2
  3.1 0.9 copy-done.2
  4.0 0.0 copy-start.3
  4.0 0.9 copy-done.3
  5.0 0.0 copy-start.6
  5.0 0.7 copy-done.6
  5.6 49.2 %shard_map.102.kv_ref = bf16[40,128,512]{2,1,0:T(8,128)(2,1)S(1)} custom-call(s32[384]{0:T(512)S(1)} %reshape.14.blocks_ref, s32[64]{0:T(128)S(1)} %copy-done.6, bf16[512,256]{1,0:T(8,128)(2,1)S(1)} %copy-done.2, bf16[512,256]{1,0:T(8,128)(2,1)S(1)} %copy-done.3), custom_call_target="tpu_custom_call" | custom-call | tf_op jit(solution)/shard_map/pallas_call | solution.py:544
  54.8 0.0 copy-done.4
  54.8 0.0 copy-start
  54.8 2.3 %copy-done = bf16[40,128,512]{2,1,0:T(8,128)(2,1)} copy-done((bf16[40,128,512]{2,1,0:T(8,128)(2,1)}, bf16[40,128,512]{2,1,0:T(8,128)(2,1)S(1)}, u32[]{:S(2)}) %copy-start) | copy-done | bytes 5242904
  57.1 0.0 copy-start.7
  57.1 28.6 %shard_map.103 = (bf16[512,2048]{1,0:T(8,128)(2,1)}, bf16[512,2048]{1,0:T(8,128)(2,1)}, bf16[40,128,512]{2,1,0:T(8,128)(2,1)}) custom-call(s32[384]{0:T(512)} %copy-done.4, s32[64]{0:T(128)} %count_ref.5, s32[384]{0:T(512)} %reshape.15.len_ref, bf16[512,2048]{1,0:T(8,128)(2,1)} %q_ref.1, bf16[512,2048]{1,0:T(8,128)(2,1)} %do_ref.1, bf16[40,128,512]{2,1,0:T(8,128)(2,1)} %copy-done), custom_call_target="tpu_custom_call" | custom-call | tf_op jit(solution)/shard_map/pallas_call | solution.py:502
  85.7 0.0 copy-done.7
  85.7 0.0 copy-start.1
  85.7 2.5 %copy-done.1 = bf16[40,128,512]{2,1,0:T(8,128)(2,1)S(1)} copy-done((bf16[40,128,512]{2,1,0:T(8,128)(2,1)S(1)}, bf16[40,128,512]{2,1,0:T(8,128)(2,1)}, u32[]{:S(2)}) %copy-start.1) | copy-done | bytes 5242904
  88.2 0.0 copy-start.5
  88.2 0.7 copy-done.5
  88.9 84.9 %shard_map.104 = (bf16[512,256]{1,0:T(8,128)(2,1)S(1)}, bf16[512,256]{1,0:T(8,128)(2,1)S(1)}) custom-call(s32[384]{0:T(512)S(1)} %copy-done.5, s32[64]{0:T(128)S(1)} %copy-done.7, bf16[40,128,512]{2,1,0:T(8,128)(2,1)S(1)} %copy-done.1), custom_call_target="tpu_custom_call" | custom-call | tf_op jit(solution)/shard_map/pallas_call | solution.py:570
  173.8 0.7 copy.15
  174.5 0.7 copy.16
Async XLA Ops:
  1.5 53.3 %copy-start.4 = (s32[384]{0:T(512)}, s32[384]{0:T(512)S(1)}, u32[]{:S(2)}) copy-start(s32[384]{0:T(512)S(1)} %reshape.14.blocks_ref) | copy-start | bytes 4612
  3.1 0.9 copy-start.2
  4.0 0.9 copy-start.3
  5.0 0.7 copy-start.6
  54.8 2.3 %copy-start = (bf16[40,128,512]{2,1,0:T(8,128)(2,1)}, bf16[40,128,512]{2,1,0:T(8,128)(2,1)S(1)}, u32[]{:S(2)}) copy-start(bf16[40,128,512]{2,1,0:T(8,128)(2,1)S(1)} %shard_map.102.kv_ref) | copy-start | bytes 15728644
  57.1 28.6 %copy-start.7 = (s32[64]{0:T(128)S(1)}, s32[64]{0:T(128)}, u32[]{:S(2)}) copy-start(s32[64]{0:T(128)} %count_ref.5) | copy-start | bytes 772
  85.7 2.5 %copy-start.1 = (bf16[40,128,512]{2,1,0:T(8,128)(2,1)S(1)}, bf16[40,128,512]{2,1,0:T(8,128)(2,1)}, u32[]{:S(2)}) copy-start(bf16[40,128,512]{2,1,0:T(8,128)(2,1)} %get-tuple-element.11.part_ref) | copy-start | bytes 15728644
  88.2 0.7 copy-start.5

commit v4 on v2

v4 whole, which is shorter than its diff:
```python
import functools
import math

import jax
import jax.numpy as jnp
from jax import lax
from jax.experimental import pallas as pl
from jax.experimental.pallas import tpu as pltpu
from jax.sharding import PartitionSpec as P

D = 128
BLOCK = 128
PER = 4
SIDE = 4
CTX = SIDE * SIDE
VIS = 6
CAP = 2
ROW = SIDE * PER
HELD = ROW + CAP * SIDE * (SIDE - 1)
STEPS = 2 * SIDE - 1
NEG = -1e30
INV_ROOT = 1.0 / math.sqrt(D)
EXP2_SCALE = INV_ROOT * math.log2(math.e)
MIB = 1 << 20
MESH = pl.DeviceIdType.MESH


def coords():
    me = lax.axis_index("ctx")
    return me, me // SIDE, lax.rem(me, SIDE)


def at(y, z):
    return {"ctx": lax.rem(y + SIDE, SIDE) * SIDE + z}


def barrier_neighbours(y, z):
    barrier = pltpu.get_barrier_semaphore()

    def greet(where):
        pl.semaphore_signal(barrier, inc=1, device_id=where, device_id_type=MESH)

    greet(at(y + 1, z))
    greet(at(y - 1, z))
    pl.when(z > 0)(lambda: greet(at(y, z - 1)))
    pl.when(z < SIDE - 1)(lambda: greet(at(y, z + 1)))
    pl.semaphore_wait(barrier, 2 + jnp.where(z > 0, 1, 0) + jnp.where(z < SIDE - 1, 1, 0))


def far_at(y, z):
    return pl.ds(ROW + (y * SIDE + z) * CAP, CAP)


def nth(n, z):
    d = (n + 1) // 2
    return z + jnp.where(lax.rem(n, 2) == 1, -d, d), d


def prep_kernel(blocks_ref, count_ref, len_ref, picks, place, seen, slot_of, low):
    me, y, z = coords()

    @pl.loop(0, SIDE * SIDE)
    def _(k):
        dst = (k // SIDE) * SIDE + z
        src = y * SIDE + lax.rem(k, SIDE)
        first, last = jnp.int32(PER - 1), jnp.int32(0)
        for r in range(PER):
            row = dst * PER + r
            count = count_ref[row]
            for s in range(1, VIS):
                t = blocks_ref[row, s] - src * PER
                hit = (t >= 0) & (t < PER) & (s < count)
                first = jnp.minimum(first, jnp.where(hit, t, PER - 1))
                last = jnp.maximum(last, jnp.where(hit, t, 0))
        picks[2 * k] = first
        picks[2 * k + 1] = last

    @pl.loop(0, PER * HELD)
    def _(n):
        slot_of[n] = -1

    for src in range(CTX):
        low[src] = PER
    for r in range(PER):
        for s in range(1, VIS):
            block = blocks_ref[me * PER + r, s]
            src = block // PER
            live = s < count_ref[me * PER + r]
            low[src] = jnp.where(live, jnp.minimum(low[src], block - src * PER), low[src])
    for r in range(PER):
        own = z * PER + r
        place[r * VIS] = own
        seen[r * VIS] = BLOCK
        slot_of[own * PER + r] = r * VIS
        for s in range(1, VIS):
            block = blocks_ref[me * PER + r, s]
            live = s < count_ref[me * PER + r]
            src = block // PER
            t = block - src * PER
            far = ROW + CAP * src + jnp.where(t == low[src], 0, 1)
            near = lax.rem(src, SIDE) * PER + t
            there = jnp.where(src // SIDE == y, near, far)
            place[r * VIS + s] = jnp.where(live, there, own)
            seen[r * VIS + s] = jnp.where(live, len_ref[me * PER + r, s], 0)

            @pl.when(live)
            def _():
                slot_of[there * PER + r] = r * VIS + s


class Attention:
    def __init__(self, head, place, seen, q_ref, do_ref, held_ref, attn_ref, dq_ref, slots_ref, scratch):
        self.place, self.seen = place, seen
        self.attn_ref, self.dq_ref, self.slots_ref = attn_ref, dq_ref, slots_ref
        (self.q, self.do, self.held, self.qs, self.dos, self.qt, self.dot, self.keys, self.values,
         self.scores, sem) = scratch
        lanes = self.q.shape[1]
        columns = pl.ds(head * lanes, lanes)
        self.loads = (
            pltpu.make_async_copy(q_ref.at[:, columns], self.q, sem.at[0]),
            pltpu.make_async_copy(do_ref.at[:, columns], self.do, sem.at[1]),
            pltpu.make_async_copy(held_ref, self.held, sem.at[2]),
        )

    @staticmethod
    def scratch(tokens, lanes):
        f32, bf16 = jnp.float32, jnp.bfloat16
        return [
            pltpu.VMEM((tokens, lanes), bf16),
            pltpu.VMEM((tokens, lanes), bf16),
            pltpu.VMEM((HELD, BLOCK, 2 * D), bf16),
            pltpu.VMEM((lanes, D), bf16),
            pltpu.VMEM((lanes, D), bf16),
            pltpu.VMEM((D, lanes), bf16),
            pltpu.VMEM((D, lanes), bf16),
            pltpu.VMEM((VIS * BLOCK, D), bf16),
            pltpu.VMEM((VIS * BLOCK, D), bf16),
            pltpu.VMEM((VIS * BLOCK, lanes), f32),
            pltpu.SemaphoreType.DMA((3,)),
        ]

    def start(self):
        for load in self.loads:
            load.start()

    def wait(self):
        for load in self.loads:
            load.wait()

    def unit(self, i):
        f32, bf16 = jnp.float32, jnp.bfloat16
        lanes = self.q.shape[1]
        tokens = pl.ds(pl.multiple_of(i * BLOCK, BLOCK), BLOCK)
        for h in range(lanes // D):
            part = slice(h * D, (h + 1) * D)
            q, do = self.q[tokens, part], self.do[tokens, part]
            self.qs[part, :] = q
            self.dos[part, :] = do
            self.qt[:, part] = q.T
            self.dot[:, part] = do.T
        for s in range(VIS):
            block = self.held[self.place[i * VIS + s]]
            rows = slice(s * BLOCK, (s + 1) * BLOCK)
            self.keys[rows, :] = block[:, :D]
            self.values[rows, :] = block[:, D:]

        tn = (((0,), (0,)), ((), ()))
        key_pos = lax.broadcasted_iota(jnp.int32, (BLOCK, lanes), 0)
        query_pos = lax.broadcasted_iota(jnp.int32, (BLOCK, lanes), 1) & (BLOCK - 1)
        pairs = [slice(p * 2 * BLOCK, (p + 1) * 2 * BLOCK) for p in range(VIS // 2)]
        top = jnp.full((1, lanes), NEG, f32)
        for p, rows in enumerate(pairs):
            raw = jnp.dot(self.keys[rows, :], self.qt[...], preferred_element_type=f32)
            first = key_pos <= query_pos if p == 0 else key_pos < self.seen[i * VIS + 2 * p]
            second = key_pos < self.seen[i * VIS + 2 * p + 1]
            raw = jnp.where(jnp.concatenate([first, second], axis=0), raw, NEG)
            self.scores[rows, :] = raw
            top = jnp.maximum(top, jnp.max(raw, axis=0, keepdims=True))
        shift = top * EXP2_SCALE
        total = jnp.zeros((1, lanes), f32)
        for rows in pairs:
            w = jnp.exp2(self.scores[rows, :] * EXP2_SCALE - shift)
            self.scores[rows, :] = w
            total = total + jnp.sum(w, axis=0, keepdims=True)
        scale = 1.0 / total
        attn = jnp.zeros((D, lanes), f32)
        for p, rows in enumerate(pairs):
            probs = self.scores[rows, :] * scale
            self.scores[rows, :] = probs
            probs = probs.astype(bf16)
            product = jnp.dot(probs, self.dos[...], preferred_element_type=f32).astype(bf16)
            self.slots_ref[i * VIS + 2 * p, :, D:] = product[:BLOCK]
            self.slots_ref[i * VIS + 2 * p + 1, :, D:] = product[BLOCK:]
            attn = attn + lax.dot_general(self.values[rows, :], probs, tn, preferred_element_type=f32)
        delta = jnp.sum(attn * self.dot[...].astype(f32), axis=0, keepdims=True)
        dq = jnp.zeros((D, lanes), f32)
        for p, rows in enumerate(pairs):
            dprobs = jnp.dot(self.values[rows, :], self.dot[...], preferred_element_type=f32)
            ds = (self.scores[rows, :] * (dprobs - delta)).astype(bf16)
            product = (jnp.dot(ds, self.qs[...], preferred_element_type=f32) * INV_ROOT).astype(bf16)
            self.slots_ref[i * VIS + 2 * p, :, :D] = product[:BLOCK]
            self.slots_ref[i * VIS + 2 * p + 1, :, :D] = product[BLOCK:]
            dq = dq + lax.dot_general(self.keys[rows, :], ds, tn, preferred_element_type=f32)
        for h in range(lanes // D):
            part = slice(h * D, (h + 1) * D)
            self.attn_ref[tokens, part] = attn[:, part].astype(bf16).T
            self.dq_ref[tokens, part] = (dq[:, part] * INV_ROOT).astype(bf16).T


def exchange_scratch(sems):
    bf16 = jnp.bfloat16
    return [
        pltpu.VMEM((SIDE, PER, BLOCK, 2 * D), bf16),
        pltpu.VMEM((SIDE, SIDE, CAP, BLOCK, 2 * D), bf16),
        pltpu.VMEM((SIDE, CAP, BLOCK, 2 * D), bf16),
        sems(SIDE),
        sems(SIDE),
        sems(SIDE),
        sems(CTX),
        sems(CTX),
        sems(SIDE),
        sems(SIDE),
        sems(SIDE),
        sems(2),
    ]


def exchange(head, picks_ref, k_ref, v_ref, out_ref, scratch, attention):
    row, packed, relay, z_recv, up_send, down_send, far_recv, y_send, relay_recv, relay_send, keep_sem, in_sem = scratch
    me, y, z = coords()
    columns = pl.ds(head * D, D)
    mine_in = (
        pltpu.make_async_copy(k_ref.at[:, :, columns], row.at[z, :, :, pl.ds(0, D)], in_sem.at[0]),
        pltpu.make_async_copy(v_ref.at[:, :, columns], row.at[z, :, :, pl.ds(D, D)], in_sem.at[1]),
    )
    for copy in mine_in:
        copy.start()
    if attention:
        attention.start()
    barrier_neighbours(y, z)
    for copy in mine_in:
        copy.wait()

    def z_copy(zs, to, sems):
        return pltpu.make_async_remote_copy(
            src_ref=row.at[zs],
            dst_ref=row.at[zs],
            send_sem=sems.at[zs],
            recv_sem=z_recv.at[zs],
            device_id=at(y, to),
            device_id_type=MESH,
        )

    def y_near(yd, zs):
        return pltpu.make_async_remote_copy(
            src_ref=packed.at[yd, zs],
            dst_ref=out_ref.at[far_at(y, zs)],
            send_sem=y_send.at[yd * SIDE + zs],
            recv_sem=far_recv.at[y * SIDE + zs],
            device_id=at(yd, z),
            device_id_type=MESH,
        )

    def y_far(yd, zs):
        return pltpu.make_async_remote_copy(
            src_ref=packed.at[yd, zs],
            dst_ref=relay.at[zs],
            send_sem=y_send.at[yd * SIDE + zs],
            recv_sem=relay_recv.at[zs],
            device_id=at(jnp.where(y == 0, SIDE - 1, 2), z),
            device_id_type=MESH,
        )

    def relay_copy(zs):
        return pltpu.make_async_remote_copy(
            src_ref=relay.at[zs],
            dst_ref=out_ref.at[far_at(3 - y, zs)],
            send_sem=relay_send.at[zs],
            recv_sem=far_recv.at[(3 - y) * SIDE + zs],
            device_id=at(5 - y, z),
            device_id_type=MESH,
        )

    def keep(zs):
        return pltpu.make_async_copy(row.at[zs], out_ref.at[pl.ds(zs * PER, PER)], keep_sem.at[zs])

    def wanted(zs):
        inside = (zs >= 0) & (zs < SIDE)
        return inside, inside & ((zs <= z) | (y < SIDE - 1))

    def pack(yd, zs):
        for c in range(CAP):
            pick = picks_ref[(yd * SIDE + zs) * CAP + c]
            block = row[zs, 0]
            for t in range(1, PER):
                block = jnp.where(pick == t, row[zs, t], block)
            packed[yd, zs, c] = block

    def step(n):
        zs, d = nth(n, z)
        inside, mine = wanted(zs)

        @pl.when(mine)
        def _():
            pl.when(d > 0)(lambda: z_copy(zs, z, up_send).wait_recv())
            pl.when((zs <= z) & (z < SIDE - 1))(lambda: z_copy(zs, z + 1, up_send).start())
            pl.when((zs >= z) & (z > 0) & (y < SIDE - 1))(
                lambda: z_copy(zs, z - 1, down_send).start()
            )
            keep(zs).start()

        @pl.when(inside)
        def _():
            @pl.loop(0, SIDE - 1 - y)
            def _(h):
                hop = jnp.where(y == 2, 1, jnp.where(h == 0, 2, jnp.where(h == 1, 1, 3)))
                yd = y + hop
                pack(yd, zs)
                pl.when(hop == 2)(lambda: y_far(yd, zs).start())
                pl.when(hop != 2)(lambda: y_near(yd, zs).start())

    def relay_step(n):
        zs, _ = nth(n, z)

        @pl.when((zs >= 0) & (zs < SIDE) & (y >= 2))
        def _():
            pltpu.make_async_remote_copy(
                src_ref=relay.at[zs],
                dst_ref=relay.at[zs],
                send_sem=relay_send.at[zs],
                recv_sem=relay_recv.at[zs],
                device_id=at(y, z),
                device_id_type=MESH,
            ).wait_recv()
            relay_copy(zs).start()

    def both(n):
        pl.when(n < STEPS)(lambda: step(n))
        pl.when((n > 0) & (n <= STEPS))(lambda: relay_step(n - 1))

    if attention:
        both(jnp.int32(0))
        attention.wait()

        @pl.loop(0, PER)
        def _(u):
            attention.unit(u)

            @pl.loop(2 * u + 1, 2 * u + 3)
            def _(n):
                both(n)
    else:
        pl.loop(0, STEPS + 1)(both)

    @pl.loop(0, y * SIDE)
    def _(n):
        pltpu.make_async_remote_copy(
            src_ref=packed.at[0, 0],
            dst_ref=out_ref.at[pl.ds(ROW + n * CAP, CAP)],
            send_sem=relay_send.at[0],
            recv_sem=far_recv.at[n],
            device_id=at(y, z),
            device_id_type=MESH,
        ).wait_recv()

    @pl.loop(0, SIDE)
    def _(zs):
        _, mine = wanted(zs)

        @pl.when(mine)
        def _():
            pl.when((zs <= z) & (z < SIDE - 1))(lambda: z_copy(zs, z + 1, up_send).wait_send())
            pl.when((zs >= z) & (z > 0) & (y < SIDE - 1))(
                lambda: z_copy(zs, z - 1, down_send).wait_send()
            )
            keep(zs).wait()

        @pl.loop(y + 1, SIDE)
        def _(yd):
            y_near(yd, zs).wait_send()

        pl.when(y >= 2)(lambda: relay_copy(zs).wait_send())


def return_scratch(sems):
    bf16 = jnp.bfloat16
    return [
        pltpu.VMEM((SIDE * (SIDE - 1), CAP, BLOCK, 2 * D), bf16),
        pltpu.VMEM((SIDE, SIDE, CAP, BLOCK, 2 * D), bf16),
        pltpu.VMEM((SIDE, CAP, BLOCK, 2 * D), bf16),
        pltpu.VMEM((SIDE, PER, BLOCK, 2 * D), bf16),
        pltpu.VMEM((SIDE, PER, BLOCK, 2 * D), bf16),
        pltpu.VMEM((SIDE, PER, BLOCK, 2 * D), bf16),
        pltpu.VMEM((PER, BLOCK, 2 * D), jnp.float32),
        sems(CTX),
        sems(CTX),
        sems(SIDE),
        sems(SIDE),
        sems(SIDE),
        sems(SIDE),
        sems(SIDE),
    ]


def give_back(picks_ref, slot_of, slots_ref, write, scratch, attention):
    (far, landed, relay, running, from_left, from_right, total,
     y_send, y_recv, relay_send, relay_recv, z_send, left_recv, right_recv) = scratch
    me, y, z = coords()
    if attention:
        attention.start()
    barrier_neighbours(y, z)

    def gathered(e):
        out = jnp.zeros((BLOCK, 2 * D), jnp.float32)
        for r in range(PER):
            slot = slot_of[e * PER + r]
            got = slots_ref[jnp.maximum(slot, 0)]
            out = out + jnp.where(slot >= 0, got, jnp.zeros_like(got)).astype(jnp.float32)
        return out

    def y_near(ys, zs):
        return pltpu.make_async_remote_copy(
            src_ref=far.at[ys * SIDE + zs],
            dst_ref=landed.at[y, zs],
            send_sem=y_send.at[ys * SIDE + zs],
            recv_sem=y_recv.at[y * SIDE + zs],
            device_id=at(ys, z),
            device_id_type=MESH,
        )

    def y_far(ys, zs):
        return pltpu.make_async_remote_copy(
            src_ref=far.at[ys * SIDE + zs],
            dst_ref=relay.at[zs],
            send_sem=y_send.at[ys * SIDE + zs],
            recv_sem=relay_recv.at[zs],
            device_id=at(5 - y, z),
            device_id_type=MESH,
        )

    def relay_copy(zs):
        return pltpu.make_async_remote_copy(
            src_ref=relay.at[zs],
            dst_ref=landed.at[5 - y, zs],
            send_sem=relay_send.at[zs],
            recv_sem=y_recv.at[(5 - y) * SIDE + zs],
            device_id=at(3 - y, z),
            device_id_type=MESH,
        )

    def z_copy(zs, to, landing, sems):
        return pltpu.make_async_remote_copy(
            src_ref=running.at[zs],
            dst_ref=landing.at[zs],
            send_sem=z_send.at[zs],
            recv_sem=sems.at[zs],
            device_id=at(y, to),
            device_id_type=MESH,
        )

    def inside(zs):
        return (zs >= 0) & (zs < SIDE)

    @pl.loop(0, STEPS)
    def _(n):
        zs, _ = nth(STEPS - 1 - n, z)

        @pl.when(inside(zs))
        def _():
            @pl.loop(0, y)
            def _(h):
                hop = jnp.where(y == 1, 1, jnp.where(h == 0, 2, jnp.where(h == 1, 1, 3)))
                ys = y - hop
                for c in range(CAP):
                    far[ys * SIDE + zs, c] = gathered(ROW + (ys * SIDE + zs) * CAP + c).astype(far.dtype)
                pl.when(hop == 2)(lambda: y_far(ys, zs).start())
                pl.when(hop != 2)(lambda: y_near(ys, zs).start())

    def relay_step(n):
        zs, _ = nth(n, z)

        @pl.when(inside(zs) & (y >= 2))
        def _():
            pltpu.make_async_remote_copy(
                src_ref=relay.at[zs],
                dst_ref=relay.at[zs],
                send_sem=relay_send.at[zs],
                recv_sem=relay_recv.at[zs],
                device_id=at(y, z),
                device_id_type=MESH,
            ).wait_recv()
            relay_copy(zs).start()

    def step(n):
        zs, d = nth(n, z)

        @pl.when(inside(zs) & ((zs <= z) | (y < SIDE - 1)))
        def _():
            for t in range(PER):
                total[t] = gathered(zs * PER + t)

            @pl.loop(y + 1, SIDE)
            def _(yd):
                pltpu.make_async_remote_copy(
                    src_ref=landed.at[yd, zs],
                    dst_ref=landed.at[yd, zs],
                    send_sem=relay_send.at[0],
                    recv_sem=y_recv.at[yd * SIDE + zs],
                    device_id=at(y, z),
                    device_id_type=MESH,
                ).wait_recv()
                for t in range(PER):
                    low, high = landed[yd, zs, 0], landed[yd, zs, 1]
                    got = jnp.where(picks_ref[(yd * SIDE + zs) * CAP + 1] == t, high, jnp.zeros_like(high))
                    got = jnp.where(picks_ref[(yd * SIDE + zs) * CAP] == t, low, got)
                    total[t] += got.astype(jnp.float32)

            @pl.when((zs <= z) & (z < SIDE - 1))
            def _():
                z_copy(zs, z, from_right, right_recv).wait_recv()
                total[...] += from_right[zs].astype(jnp.float32)

            @pl.when((zs >= z) & (z > 0) & (y < SIDE - 1))
            def _():
                z_copy(zs, z, from_left, left_recv).wait_recv()
                total[...] += from_left[zs].astype(jnp.float32)

            @pl.when(d > 0)
            def _():
                running[zs] = total[...].astype(running.dtype)
                pl.when(zs < z)(lambda: z_copy(zs, z - 1, from_right, right_recv).start())
                pl.when(zs > z)(lambda: z_copy(zs, z + 1, from_left, left_recv).start())

    def relay_nth(n):
        pl.when((n >= 0) & (n < STEPS))(lambda: relay_step(STEPS - 1 - n))

    def step_nth(n):
        pl.when((n >= 0) & (n < STEPS))(lambda: step(STEPS - 1 - n))

    if attention:
        attention.wait()

        @pl.loop(0, PER)
        def _(u):
            attention.unit(u)

            @pl.loop(2 * u, 2 * u + 2)
            def _(n):
                step_nth(n - 2)
                relay_nth(n)

        step_nth(jnp.int32(STEPS - 1))
    else:

        @pl.loop(0, STEPS)
        def _(n):
            relay_nth(n)
            step_nth(n)

    write(total)

    @pl.loop(0, SIDE)
    def _(zs):
        pl.when((zs < z) | ((zs > z) & (y < SIDE - 1)))(
            lambda: z_copy(zs, z, from_right, right_recv).wait_send()
        )

        @pl.loop(0, y)
        def _(ys):
            y_near(ys, zs).wait_send()

        pl.when(y >= 2)(lambda: relay_copy(zs).wait_send())


def first_exchange(picks, k_ref, v_ref, held_ref, *scratch):
    exchange(0, picks, k_ref, v_ref, held_ref, scratch, None)


def exchange_and_attend(
    picks, place, seen, k_ref, v_ref, q_ref, do_ref, held_ref, next_ref, attn_ref, dq_ref, slots_ref, *scratch
):
    attention = Attention(0, place, seen, q_ref, do_ref, held_ref, attn_ref, dq_ref, slots_ref, scratch[:11])
    exchange(1, picks, k_ref, v_ref, next_ref, scratch[11:], attention)


def return_and_attend(
    picks, slot_of, place, seen, q_ref, do_ref, held_ref, done_ref, grads_ref, attn_ref, dq_ref, slots_ref, *scratch
):
    attention = Attention(1, place, seen, q_ref, do_ref, held_ref, attn_ref, dq_ref, slots_ref, scratch[:11])

    def write(total):
        for t in range(PER):
            grads_ref[pl.ds(t * BLOCK, BLOCK), :] = total[t].astype(grads_ref.dtype)

    give_back(picks, slot_of, done_ref, write, scratch[11:], attention)


def last_return(picks, slot_of, done_ref, grads_ref, gk_ref, gv_ref, *scratch):
    def write(total):
        gk_ref[:, :D] = grads_ref[:, :D]
        gv_ref[:, :D] = grads_ref[:, D:]
        for t in range(PER):
            rows = pl.ds(t * BLOCK, BLOCK)
            gk_ref[rows, D:] = total[t, :, :D].astype(gk_ref.dtype)
            gv_ref[rows, D:] = total[t, :, D:].astype(gv_ref.dtype)

    give_back(picks, slot_of, done_ref, write, scratch, None)


def body(query_states, key_states, value_state_rows, grad_out, vis_blocks, vis_count, vis_len):
    tokens, q_width = query_states.shape
    width = key_states.shape[1]
    lanes = q_width * D // width
    bf16, i32 = jnp.bfloat16, jnp.int32
    sems = lambda n: pltpu.SemaphoreType.DMA((n,))
    smem = pl.BlockSpec(memory_space=pltpu.SMEM)
    vmem = pl.BlockSpec(memory_space=pltpu.VMEM)
    hbm = pl.BlockSpec(memory_space=pl.ANY)
    shape = jax.ShapeDtypeStruct
    held = shape((HELD, BLOCK, 2 * D), bf16)
    half = shape((tokens, lanes), bf16)
    slots = shape((PER * VIS, BLOCK, 2 * D), bf16)
    grads = shape((tokens, 2 * D), bf16)
    whole = shape((tokens, width), bf16)

    def remote(n):
        return pltpu.CompilerParams(collective_id=n, has_side_effects=True, vmem_limit_bytes=48 * MIB)

    picks, place, seen, slot_of = pl.pallas_call(
        prep_kernel,
        out_shape=tuple(shape((n,), i32) for n in (CTX * CAP, PER * VIS, PER * VIS, PER * HELD)),
        in_specs=[smem] * 3,
        out_specs=(smem,) * 4,
        scratch_shapes=[pltpu.SMEM((CTX,), i32)],
    )(vis_blocks, vis_count, vis_len)
    keys = key_states.reshape(PER, BLOCK, width)
    values = value_state_rows.reshape(PER, BLOCK, width)

    held_0 = pl.pallas_call(
        first_exchange,
        out_shape=held,
        in_specs=[smem, hbm, hbm],
        out_specs=hbm,
        scratch_shapes=exchange_scratch(sems),
        compiler_params=remote(0),
    )(picks, keys, values)
    held_1, attn_0, dq_0, slots_0 = pl.pallas_call(
        exchange_and_attend,
        out_shape=(held, half, half, slots),
        in_specs=[smem] * 3 + [hbm] * 5,
        out_specs=(hbm, vmem, vmem, vmem),
        scratch_shapes=Attention.scratch(tokens, lanes) + exchange_scratch(sems),
        compiler_params=remote(1),
    )(picks, place, seen, keys, values, query_states, grad_out, held_0)
    grads_0, attn_1, dq_1, slots_1 = pl.pallas_call(
        return_and_attend,
        out_shape=(grads, half, half, slots),
        in_specs=[smem] * 4 + [hbm] * 3 + [vmem],
        out_specs=(vmem, vmem, vmem, vmem),
        scratch_shapes=Attention.scratch(tokens, lanes) + return_scratch(sems),
        compiler_params=remote(2),
    )(picks, slot_of, place, seen, query_states, grad_out, held_1, slots_0)
    grad_key, grad_value = pl.pallas_call(
        last_return,
        out_shape=(whole, whole),
        in_specs=[smem] * 2 + [vmem] * 2,
        out_specs=(vmem, vmem),
        scratch_shapes=return_scratch(sems),
        compiler_params=remote(3),
    )(picks, slot_of, slots_1, grads_0)
    attention = jnp.concatenate([attn_0, attn_1], axis=1)
    grad_query = jnp.concatenate([dq_0, dq_1], axis=1)
    return attention, grad_query, grad_key, grad_value


def solution(mesh):
    rows = P(("dp", "ctx"), "head")
    return jax.shard_map(
        body,
        mesh=mesh,
        in_specs=(rows, rows, rows, rows, P("dp", None), P("dp"), P("dp", None)),
        out_specs=(rows, rows, rows, rows),
        check_vma=False,
    )
```

time: 187 us -> 148 us (0.79)
  the two profiles are of different devices: /device:TPU:135 before, /device:TPU:36 now
where the time goes in v4:
time: 148 us; the launch traced here: 147 us
  Pallas kernels  136 us (92%)
  local copies, waits for them, and re-layouts  8.26 us (6%)
  other arithmetic  2.45 us (2%)
    pallas_call x1, Pallas kernels, body(): pl.pallas_call(return_and_attend, out_shape=(grads, half, half, slots), i...  44.3 us
    pallas_call x1, Pallas kernels, body(): pl.pallas_call(last_return, out_shape=(whole, whole), in_specs=[smem] * 2...  31.4 us
    pallas_call x1, Pallas kernels, body(): pl.pallas_call(exchange_and_attend, out_shape=(held, half, half, slots),...  28.2 us
    pallas_call x1, Pallas kernels, body(): pl.pallas_call(first_exchange, out_shape=held, in_specs=[smem, hbm, hbm],...  26.6 us
    unnamed x20, local copies, waits for them, and re-layouts  8.26 us
    pallas_call x1, Pallas kernels, body(): pl.pallas_call(prep_kernel, out_shape=tuple((shape((n,), i32) for n in (C...  5.45 us

profile of v4, /device:TPU:36, one launch (start us, length us, event | category | flops | bytes accessed | tf_op | source)
XLA Modules:
  0.0 147.4 jit_solution(18440226451390839066)
XLA Ops:
  0.6 1.4 copy.11.blocks_ref
  2.0 1.4 copy.12.len_ref
  3.4 5.4 %shard_map.102 = (s32[32]{0:T(128)}, s32[24]{0:T(128)}, s32[24]{0:T(128)}, s32[160]{0:T(256)}) custom-call(s32[64,6]{1,0:T(8,128)} %copy.11.blocks_ref, s32[64]{0:T(128)} %count_ref.1, s32[64,6]{1,0:T(8,128)} %copy.12.len_ref), custom_call_target="tpu_custom_call" | custom-call | tf_op jit(solution)/shard_map/pallas_call | solution.py:629
  8.9 0.0 copy-start.6
  8.9 0.0 copy-start.7
  8.9 0.0 copy-start.1
  8.9 0.9 copy-done.1
  9.8 0.0 copy-start.3
  9.8 0.9 copy-done.3
  10.8 0.0 copy-start.4
  10.8 0.7 copy-done.4
  11.4 0.0 copy-start.2
  11.4 26.6 %shard_map.103.held_ref = bf16[40,128,256]{2,1,0:T(8,128)(2,1)S(1)} custom-call(s32[32]{0:T(128)S(1)} %copy-done.4, bf16[4,128,256]{2,1,0:T(8,128)(2,1)S(1)} %bitcast.2, bf16[4,128,256]{2,1,0:T(8,128)(2,1)S(1)} %bitcast.4), custom_call_target="tpu_custom_call" | custom-call | tf_op jit(solution)/shard_map/pallas_call | solution.py:639
  38.1 0.0 copy-start
  38.1 1.5 %copy-done = bf16[40,128,256]{2,1,0:T(8,128)(2,1)} copy-done((bf16[40,128,256]{2,1,0:T(8,128)(2,1)}, bf16[40,128,256]{2,1,0:T(8,128)(2,1)S(1)}, u32[]{:S(2)}) %copy-start) | copy-done | bytes 2621464
  39.6 0.0 copy-done.6
  39.6 0.0 copy-done.7
  39.6 0.0 copy-done.2
  39.6 0.0 copy-start.5
  39.6 28.2 %shard_map.104 = (bf16[40,128,256]{2,1,0:T(8,128)(2,1)}, bf16[512,1024]{1,0:T(8,128)(2,1)S(1)}, bf16[512,1024]{1,0:T(8,128)(2,1)S(1)}, bf16[24,128,256]{2,1,0:T(8,128)(2,1)S(1)}) custom-call(s32[32]{0:T(128)S(1)} %copy-done.4, s32[24]{0:T(128)S(1)} %copy-done.6, s32[24]{0:T(128)S(1)} %copy-done.7, bf16[4,128,256]{2,1,0:T(8,128)(2,1)S(1)} %bitcast.3, ...), custom_call_target="tpu_custom_call" | custom-call | tf_op jit(solution)/shard_map/pallas_call | solution.py:647
  67.8 0.0 copy-done.5
  67.8 44.3 %shard_map.105 = (bf16[512,256]{1,0:T(8,128)(2,1)S(1)}, bf16[512,1024]{1,0:T(8,128)(2,1)S(1)}, bf16[512,1024]{1,0:T(8,128)(2,1)S(1)}, bf16[24,128,256]{2,1,0:T(8,128)(2,1)S(1)}) custom-call(s32[32]{0:T(128)S(1)} %copy-done.4, s32[160]{0:T(256)S(1)} %copy-done.5, s32[24]{0:T(128)S(1)} %copy-done.6, s32[24]{0:T(128)S(1)} %copy-done.7, ...), custom_call_target="tpu_custom_call" | custom-call | tf_op jit(solution)/shard_map/pallas_call | solution.py:655
  112.1 2.5 %pad_maximum_fusion = (bf16[512,2048]{1,0:T(8,128)(2,1)}, bf16[512,2048]{1,0:T(8,128)(2,1)}) fusion(bf16[512,1024]{1,0:T(8,128)(2,1)S(1)} %get-tuple-element.25, bf16[512,1024]{1,0:T(8,128)(2,1)S(1)} %get-tuple-element.21, bf16[512,1024]{1,0:T(8,128)(2,1)S(1)} %get-tuple-element.27, bf16[512,1024]{1,0:T(8,128)(2,1)S(1)} %get-tuple-element.26), kind=kLoop, calls=%fused_computation | loop fusion | flops 8388608 | bytes 8388608 | tf_op jit(solution)/shard_map/concatenate | solution.py:671
  114.6 31.4 %shard_map.106 = (bf16[512,256]{1,0:T(8,128)(2,1)S(1)}, bf16[512,256]{1,0:T(8,128)(2,1)S(1)}) custom-call(s32[32]{0:T(128)S(1)} %copy-done.4, s32[160]{0:T(256)S(1)} %copy-done.5, bf16[24,128,256]{2,1,0:T(8,128)(2,1)S(1)} %get-tuple-element.28.done_ref, bf16[512,256]{1,0:T(8,128)(2,1)S(1)} %get-tuple-element.29.grads_ref), custom_call_target="tpu_custom_call" | custom-call | tf_op jit(solution)/shard_map/pallas_call | solution.py:663
  145.9 0.7 copy.15
  146.7 0.7 copy.16
Async XLA Ops:
  8.9 30.7 %copy-start.6 = (s32[24]{0:T(128)S(1)}, s32[24]{0:T(128)}, u32[]{:S(2)}) copy-start(s32[24]{0:T(128)} %get-tuple-element.19.place) | copy-start | bytes 292
  8.9 30.7 %copy-start.7 = (s32[24]{0:T(128)S(1)}, s32[24]{0:T(128)}, u32[]{:S(2)}) copy-start(s32[24]{0:T(128)} %get-tuple-element.20.seen) | copy-start | bytes 292
  8.9 1.0 copy-start.1
  9.8 0.9 copy-start.3
  10.8 0.7 copy-start.4
  11.4 28.1 %copy-start.2 = (bf16[512,256]{1,0:T(8,128)(2,1)S(1)}, bf16[512,256]{1,0:T(8,128)(2,1)}, u32[]{:S(2)}) copy-start(bf16[512,256]{1,0:T(8,128)(2,1)} %param.8) | copy-start | bytes 786436
  38.1 1.5 %copy-start = (bf16[40,128,256]{2,1,0:T(8,128)(2,1)}, bf16[40,128,256]{2,1,0:T(8,128)(2,1)S(1)}, u32[]{:S(2)}) copy-start(bf16[40,128,256]{2,1,0:T(8,128)(2,1)S(1)} %shard_map.103.held_ref) | copy-start | bytes 7864324
  39.6 28.2 %copy-start.5 = (s32[160]{0:T(256)S(1)}, s32[160]{0:T(256)}, u32[]{:S(2)}) copy-start(s32[160]{0:T(256)} %get-tuple-element.22.slot_of) | copy-start | bytes 1924

commit v5 on v4

--- a/solution.py
+++ b/solution.py
@@ -18,6 +18,8 @@
 ROW = SIDE * PER
 HELD = ROW + CAP * SIDE * (SIDE - 1)
 STEPS = 2 * SIDE - 1
+PAIRS = [slice(p * 2 * BLOCK, (p + 1) * 2 * BLOCK) for p in range(VIS // 2)]
+TN = (((0,), (0,)), ((), ()))
 NEG = -1e30
 INV_ROOT = 1.0 / math.sqrt(D)
 EXP2_SCALE = INV_ROOT * math.log2(math.e)
@@ -56,56 +58,50 @@
     return z + jnp.where(lax.rem(n, 2) == 1, -d, d), d
 
 
-def prep_kernel(blocks_ref, count_ref, len_ref, picks, place, seen, slot_of, low):
+def chosen(blocks_ref, count_ref, dst, src):
+    low, high = jnp.int32(PER - 1), jnp.int32(0)
+    for r in range(PER):
+        row = dst * PER + r
+        count = count_ref[row]
+        for s in range(1, VIS):
+            t = blocks_ref[s, row] - src * PER
+            hit = (t >= 0) & (t < PER) & (s < count)
+            low = jnp.minimum(low, jnp.where(hit, t, PER - 1))
+            high = jnp.maximum(high, jnp.where(hit, t, 0))
+    return low, high
+
+
+def tables(blocks_ref, count_ref, len_ref, place, seen, slot_of):
     me, y, z = coords()
 
-    @pl.loop(0, SIDE * SIDE)
-    def _(k):
-        dst = (k // SIDE) * SIDE + z
-        src = y * SIDE + lax.rem(k, SIDE)
-        first, last = jnp.int32(PER - 1), jnp.int32(0)
-        for r in range(PER):
-            row = dst * PER + r
-            count = count_ref[row]
-            for s in range(1, VIS):
-                t = blocks_ref[row, s] - src * PER
-                hit = (t >= 0) & (t < PER) & (s < count)
-                first = jnp.minimum(first, jnp.where(hit, t, PER - 1))
-                last = jnp.maximum(last, jnp.where(hit, t, 0))
-        picks[2 * k] = first
-        picks[2 * k + 1] = last
-
-    @pl.loop(0, PER * HELD)
-    def _(n):
-        slot_of[n] = -1
-
-    for src in range(CTX):
-        low[src] = PER
-    for r in range(PER):
-        for s in range(1, VIS):
-            block = blocks_ref[me * PER + r, s]
-            src = block // PER
-            live = s < count_ref[me * PER + r]
-            low[src] = jnp.where(live, jnp.minimum(low[src], block - src * PER), low[src])
-    for r in range(PER):
+    @pl.loop(0, PER)
+    def _(r):
+        row = me * PER + r
         own = z * PER + r
         place[r * VIS] = own
         seen[r * VIS] = BLOCK
-        slot_of[own * PER + r] = r * VIS
-        for s in range(1, VIS):
-            block = blocks_ref[me * PER + r, s]
-            live = s < count_ref[me * PER + r]
+
+        @pl.loop(1, VIS)
+        def _(s):
+            block = blocks_ref[s, row]
+            live = s < count_ref[row]
             src = block // PER
             t = block - src * PER
-            far = ROW + CAP * src + jnp.where(t == low[src], 0, 1)
+            low, _ = chosen(blocks_ref, count_ref, me, src)
+            far = ROW + CAP * src + jnp.where(t == low, 0, 1)
             near = lax.rem(src, SIDE) * PER + t
             there = jnp.where(src // SIDE == y, near, far)
             place[r * VIS + s] = jnp.where(live, there, own)
-            seen[r * VIS + s] = jnp.where(live, len_ref[me * PER + r, s], 0)
-
-            @pl.when(live)
-            def _():
-                slot_of[there * PER + r] = r * VIS + s
+            seen[r * VIS + s] = jnp.where(live, len_ref[s, row], 0)
+
+    @pl.loop(0, HELD)
+    def _(e):
+        for r in range(PER):
+            slot = jnp.int32(-1)
+            for s in range(VIS):
+                hit = (place[r * VIS + s] == e) & (seen[r * VIS + s] > 0)
+                slot = jnp.where(hit, r * VIS + s, slot)
+            slot_of[e * PER + r] = slot
 
 
 class Attention:
@@ -113,7 +109,7 @@
         self.place, self.seen = place, seen
         self.attn_ref, self.dq_ref, self.slots_ref = attn_ref, dq_ref, slots_ref
         (self.q, self.do, self.held, self.qs, self.dos, self.qt, self.dot, self.keys, self.values,
-         self.scores, sem) = scratch
+         self.scores, self.scale, self.delta, sem) = scratch
         lanes = self.q.shape[1]
         columns = pl.ds(head * lanes, lanes)
         self.loads = (
@@ -136,6 +132,8 @@
             pltpu.VMEM((VIS * BLOCK, D), bf16),
             pltpu.VMEM((VIS * BLOCK, D), bf16),
             pltpu.VMEM((VIS * BLOCK, lanes), f32),
+            pltpu.VMEM((1, lanes), f32),
+            pltpu.VMEM((1, lanes), f32),
             pltpu.SemaphoreType.DMA((3,)),
         ]
 
@@ -147,7 +145,7 @@
         for load in self.loads:
             load.wait()
 
-    def unit(self, i):
+    def weigh(self, i):
         f32, bf16 = jnp.float32, jnp.bfloat16
         lanes = self.q.shape[1]
         tokens = pl.ds(pl.multiple_of(i * BLOCK, BLOCK), BLOCK)
@@ -164,12 +162,10 @@
             self.keys[rows, :] = block[:, :D]
             self.values[rows, :] = block[:, D:]
 
-        tn = (((0,), (0,)), ((), ()))
         key_pos = lax.broadcasted_iota(jnp.int32, (BLOCK, lanes), 0)
         query_pos = lax.broadcasted_iota(jnp.int32, (BLOCK, lanes), 1) & (BLOCK - 1)
-        pairs = [slice(p * 2 * BLOCK, (p + 1) * 2 * BLOCK) for p in range(VIS // 2)]
         top = jnp.full((1, lanes), NEG, f32)
-        for p, rows in enumerate(pairs):
+        for p, rows in enumerate(PAIRS):
             raw = jnp.dot(self.keys[rows, :], self.qt[...], preferred_element_type=f32)
             first = key_pos <= query_pos if p == 0 else key_pos < self.seen[i * VIS + 2 * p]
             second = key_pos < self.seen[i * VIS + 2 * p + 1]
@@ -178,33 +174,64 @@
             top = jnp.maximum(top, jnp.max(raw, axis=0, keepdims=True))
         shift = top * EXP2_SCALE
         total = jnp.zeros((1, lanes), f32)
-        for rows in pairs:
+        for rows in PAIRS:
             w = jnp.exp2(self.scores[rows, :] * EXP2_SCALE - shift)
             self.scores[rows, :] = w
             total = total + jnp.sum(w, axis=0, keepdims=True)
-        scale = 1.0 / total
+        self.scale[...] = 1.0 / total
+
+    def mix(self, i):
+        f32, bf16 = jnp.float32, jnp.bfloat16
+        lanes = self.q.shape[1]
+        scale = self.scale[...]
         attn = jnp.zeros((D, lanes), f32)
-        for p, rows in enumerate(pairs):
+        for p, rows in enumerate(PAIRS):
             probs = self.scores[rows, :] * scale
             self.scores[rows, :] = probs
             probs = probs.astype(bf16)
             product = jnp.dot(probs, self.dos[...], preferred_element_type=f32).astype(bf16)
             self.slots_ref[i * VIS + 2 * p, :, D:] = product[:BLOCK]
             self.slots_ref[i * VIS + 2 * p + 1, :, D:] = product[BLOCK:]
-            attn = attn + lax.dot_general(self.values[rows, :], probs, tn, preferred_element_type=f32)
-        delta = jnp.sum(attn * self.dot[...].astype(f32), axis=0, keepdims=True)
+            attn = attn + lax.dot_general(self.values[rows, :], probs, TN, preferred_element_type=f32)
+        self.delta[...] = jnp.sum(attn * self.dot[...].astype(f32), axis=0, keepdims=True)
+        self.put(self.attn_ref, i, attn)
+
+    def back(self, i):
+        f32, bf16 = jnp.float32, jnp.bfloat16
+        lanes = self.q.shape[1]
+        delta = self.delta[...]
         dq = jnp.zeros((D, lanes), f32)
-        for p, rows in enumerate(pairs):
+        for p, rows in enumerate(PAIRS):
             dprobs = jnp.dot(self.values[rows, :], self.dot[...], preferred_element_type=f32)
             ds = (self.scores[rows, :] * (dprobs - delta)).astype(bf16)
             product = (jnp.dot(ds, self.qs[...], preferred_element_type=f32) * INV_ROOT).astype(bf16)
             self.slots_ref[i * VIS + 2 * p, :, :D] = product[:BLOCK]
             self.slots_ref[i * VIS + 2 * p + 1, :, :D] = product[BLOCK:]
-            dq = dq + lax.dot_general(self.keys[rows, :], ds, tn, preferred_element_type=f32)
-        for h in range(lanes // D):
+            dq = dq + lax.dot_general(self.keys[rows, :], ds, TN, preferred_element_type=f32)
+        self.put(self.dq_ref, i, dq * INV_ROOT)
+
+    def put(self, ref, i, transposed):
+        tokens = pl.ds(pl.multiple_of(i * BLOCK, BLOCK), BLOCK)
+        for h in range(transposed.shape[1] // D):
             part = slice(h * D, (h + 1) * D)
-            self.attn_ref[tokens, part] = attn[:, part].astype(bf16).T
-            self.dq_ref[tokens, part] = (dq[:, part] * INV_ROOT).astype(bf16).T
+            ref[tokens, part] = transposed[:, part].astype(ref.dtype).T
+
+    def run(self, between):
+        @pl.loop(0, 3 * PER)
+        def _(k):
+            i = k // 3
+            phase = k - 3 * i
+            pl.when(phase == 0)(lambda: self.weigh(i))
+            pl.when(phase == 1)(lambda: self.mix(i))
+            pl.when(phase == 2)(lambda: self.back(i))
+            between(k)
+
+
+def listed(k, table):
+    low = high = jnp.int32(0)
+    for key, (first, last) in table.items():
+        low, high = jnp.where(k == key, first, low), jnp.where(k == key, last, high)
+    return low, high
 
 
 def exchange_scratch(sems):
@@ -225,7 +252,7 @@
     ]
 
 
-def exchange(head, picks_ref, k_ref, v_ref, out_ref, scratch, attention):
+def exchange(head, picks_ref, k_ref, v_ref, out_ref, scratch, attention, lists=None):
     row, packed, relay, z_recv, up_send, down_send, far_recv, y_send, relay_recv, relay_send, keep_sem, in_sem = scratch
     me, y, z = coords()
     columns = pl.ds(head * D, D)
@@ -289,8 +316,14 @@
         return inside, inside & ((zs <= z) | (y < SIDE - 1))
 
     def pack(yd, zs):
+        first = (yd * SIDE + zs) * CAP
+        if lists:
+            blocks_ref, count_ref = lists[:2]
+            picks_ref[first], picks_ref[first + 1] = chosen(
+                blocks_ref, count_ref, yd * SIDE + z, y * SIDE + zs
+            )
         for c in range(CAP):
-            pick = picks_ref[(yd * SIDE + zs) * CAP + c]
+            pick = picks_ref[first + c]
             block = row[zs, 0]
             for t in range(1, PER):
                 block = jnp.where(pick == t, row[zs, t], block)
@@ -334,23 +367,22 @@
             ).wait_recv()
             relay_copy(zs).start()
 
-    def both(n):
-        pl.when(n < STEPS)(lambda: step(n))
-        pl.when((n > 0) & (n <= STEPS))(lambda: relay_step(n - 1))
-
+    step(jnp.int32(0))
     if attention:
-        both(jnp.int32(0))
         attention.wait()
 
-        @pl.loop(0, PER)
-        def _(u):
-            attention.unit(u)
-
-            @pl.loop(2 * u + 1, 2 * u + 3)
-            def _(n):
-                both(n)
+        def between(k):
+            pl.loop(*listed(k, {1: (1, 3), 4: (3, 5), 7: (5, 7)}))(step)
+            pl.loop(*listed(k, {1: (0, 1), 4: (1, 3), 7: (3, 5), 9: (5, 7)}))(relay_step)
+
+        attention.run(between)
     else:
-        pl.loop(0, STEPS + 1)(both)
+        tables(*lists)
+
+        @pl.loop(1, STEPS + 1)
+        def _(n):
+            pl.when(n < STEPS)(lambda: step(n))
+            relay_step(n - 1)
 
     @pl.loop(0, y * SIDE)
     def _(n):
@@ -396,9 +428,9 @@
         sems(CTX),
         sems(SIDE),
         sems(SIDE),
-        sems(SIDE),
-        sems(SIDE),
-        sems(SIDE),
+        sems(2 * SIDE),
+        sems(2 * SIDE),
+        sems(2 * SIDE),
     ]
 
 
@@ -448,12 +480,13 @@
             device_id_type=MESH,
         )
 
-    def z_copy(zs, to, landing, sems):
+    def z_copy(zs, half, to, landing, sems):
+        blocks = pl.ds(2 * half, 2)
         return pltpu.make_async_remote_copy(
-            src_ref=running.at[zs],
-            dst_ref=landing.at[zs],
-            send_sem=z_send.at[zs],
-            recv_sem=sems.at[zs],
+            src_ref=running.at[zs, blocks],
+            dst_ref=landing.at[zs, blocks],
+            send_sem=z_send.at[2 * zs + half],
+            recv_sem=sems.at[2 * zs + half],
             device_id=at(y, to),
             device_id_type=MESH,
         )
@@ -515,41 +548,40 @@
                     got = jnp.where(picks_ref[(yd * SIDE + zs) * CAP] == t, low, got)
                     total[t] += got.astype(jnp.float32)
 
-            @pl.when((zs <= z) & (z < SIDE - 1))
-            def _():
-                z_copy(zs, z, from_right, right_recv).wait_recv()
-                total[...] += from_right[zs].astype(jnp.float32)
-
-            @pl.when((zs >= z) & (z > 0) & (y < SIDE - 1))
-            def _():
-                z_copy(zs, z, from_left, left_recv).wait_recv()
-                total[...] += from_left[zs].astype(jnp.float32)
-
-            @pl.when(d > 0)
-            def _():
-                running[zs] = total[...].astype(running.dtype)
-                pl.when(zs < z)(lambda: z_copy(zs, z - 1, from_right, right_recv).start())
-                pl.when(zs > z)(lambda: z_copy(zs, z + 1, from_left, left_recv).start())
+            @pl.loop(0, 2)
+            def _(half):
+                blocks = pl.ds(2 * half, 2)
+
+                @pl.when((zs <= z) & (z < SIDE - 1))
+                def _():
+                    z_copy(zs, half, z, from_right, right_recv).wait_recv()
+                    total[blocks] += from_right[zs, blocks].astype(jnp.float32)
+
+                @pl.when((zs >= z) & (z > 0) & (y < SIDE - 1))
+                def _():
+                    z_copy(zs, half, z, from_left, left_recv).wait_recv()
+                    total[blocks] += from_left[zs, blocks].astype(jnp.float32)
+
+                @pl.when(d > 0)
+                def _():
+                    running[zs, blocks] = total[blocks].astype(running.dtype)
+                    pl.when(zs < z)(lambda: z_copy(zs, half, z - 1, from_right, right_recv).start())
+                    pl.when(zs > z)(lambda: z_copy(zs, half, z + 1, from_left, left_recv).start())
 
     def relay_nth(n):
-        pl.when((n >= 0) & (n < STEPS))(lambda: relay_step(STEPS - 1 - n))
+        relay_step(STEPS - 1 - n)
 
     def step_nth(n):
-        pl.when((n >= 0) & (n < STEPS))(lambda: step(STEPS - 1 - n))
+        step(STEPS - 1 - n)
 
     if attention:
         attention.wait()
 
-        @pl.loop(0, PER)
-        def _(u):
-            attention.unit(u)
-
-            @pl.loop(2 * u, 2 * u + 2)
-            def _(n):
-                step_nth(n - 2)
-                relay_nth(n)
-
-        step_nth(jnp.int32(STEPS - 1))
+        def between(k):
+            pl.loop(*listed(k, {2: (0, 2), 4: (2, 4), 6: (4, 6), 8: (6, 7)}))(step_nth)
+            pl.loop(*listed(k, {1: (0, 2), 2: (2, 4), 4: (4, 6), 6: (6, 7)}))(relay_nth)
+
+        attention.run(between)
     else:
 
         @pl.loop(0, STEPS)
@@ -561,9 +593,10 @@
 
     @pl.loop(0, SIDE)
     def _(zs):
-        pl.when((zs < z) | ((zs > z) & (y < SIDE - 1)))(
-            lambda: z_copy(zs, z, from_right, right_recv).wait_send()
-        )
+        @pl.when((zs < z) | ((zs > z) & (y < SIDE - 1)))
+        def _():
+            for half in range(2):
+                z_copy(zs, half, z, from_right, right_recv).wait_send()
 
         @pl.loop(0, y)
         def _(ys):
@@ -572,27 +605,30 @@
         pl.when(y >= 2)(lambda: relay_copy(zs).wait_send())
 
 
-def first_exchange(picks, k_ref, v_ref, held_ref, *scratch):
-    exchange(0, picks, k_ref, v_ref, held_ref, scratch, None)
+def first_exchange(
+    blocks_ref, count_ref, len_ref, k_ref, v_ref, held_ref, picks, place, seen, slot_of, *scratch
+):
+    lists = (blocks_ref, count_ref, len_ref, place, seen, slot_of)
+    exchange(0, picks, k_ref, v_ref, held_ref, scratch, None, lists)
 
 
 def exchange_and_attend(
     picks, place, seen, k_ref, v_ref, q_ref, do_ref, held_ref, next_ref, attn_ref, dq_ref, slots_ref, *scratch
 ):
-    attention = Attention(0, place, seen, q_ref, do_ref, held_ref, attn_ref, dq_ref, slots_ref, scratch[:11])
-    exchange(1, picks, k_ref, v_ref, next_ref, scratch[11:], attention)
+    attention = Attention(0, place, seen, q_ref, do_ref, held_ref, attn_ref, dq_ref, slots_ref, scratch[:13])
+    exchange(1, picks, k_ref, v_ref, next_ref, scratch[13:], attention)
 
 
 def return_and_attend(
     picks, slot_of, place, seen, q_ref, do_ref, held_ref, done_ref, grads_ref, attn_ref, dq_ref, slots_ref, *scratch
 ):
-    attention = Attention(1, place, seen, q_ref, do_ref, held_ref, attn_ref, dq_ref, slots_ref, scratch[:11])
+    attention = Attention(1, place, seen, q_ref, do_ref, held_ref, attn_ref, dq_ref, slots_ref, scratch[:13])
 
     def write(total):
         for t in range(PER):
             grads_ref[pl.ds(t * BLOCK, BLOCK), :] = total[t].astype(grads_ref.dtype)
 
-    give_back(picks, slot_of, done_ref, write, scratch[11:], attention)
+    give_back(picks, slot_of, done_ref, write, scratch[13:], attention)
 
 
 def last_return(picks, slot_of, done_ref, grads_ref, gk_ref, gv_ref, *scratch):
@@ -611,11 +647,11 @@
     tokens, q_width = query_states.shape
     width = key_states.shape[1]
     lanes = q_width * D // width
-    bf16, i32 = jnp.bfloat16, jnp.int32
+    bf16 = jnp.bfloat16
     sems = lambda n: pltpu.SemaphoreType.DMA((n,))
     smem = pl.BlockSpec(memory_space=pltpu.SMEM)
     vmem = pl.BlockSpec(memory_space=pltpu.VMEM)
-    hbm = pl.BlockSpec(memory_space=pl.ANY)
+    hbm = pl.BlockSpec(memory_space=pltpu.HBM)
     shape = jax.ShapeDtypeStruct
     held = shape((HELD, BLOCK, 2 * D), bf16)
     half = shape((tokens, lanes), bf16)
@@ -624,26 +660,20 @@
     whole = shape((tokens, width), bf16)
 
     def remote(n):
-        return pltpu.CompilerParams(collective_id=n, has_side_effects=True, vmem_limit_bytes=48 * MIB)
-
-    picks, place, seen, slot_of = pl.pallas_call(
-        prep_kernel,
-        out_shape=tuple(shape((n,), i32) for n in (CTX * CAP, PER * VIS, PER * VIS, PER * HELD)),
-        in_specs=[smem] * 3,
-        out_specs=(smem,) * 4,
-        scratch_shapes=[pltpu.SMEM((CTX,), i32)],
-    )(vis_blocks, vis_count, vis_len)
+        return pltpu.CompilerParams(collective_id=n, has_side_effects=True, vmem_limit_bytes=56 * MIB)
+
     keys = key_states.reshape(PER, BLOCK, width)
     values = value_state_rows.reshape(PER, BLOCK, width)
 
-    held_0 = pl.pallas_call(
+    sizes = (CTX * CAP, PER * VIS, PER * VIS, PER * HELD)
+    held_0, picks, place, seen, slot_of = pl.pallas_call(
         first_exchange,
-        out_shape=held,
-        in_specs=[smem, hbm, hbm],
-        out_specs=hbm,
+        out_shape=(held,) + tuple(shape((n,), jnp.int32) for n in sizes),
+        in_specs=[smem] * 3 + [hbm] * 2,
+        out_specs=(hbm,) + (smem,) * 4,
         scratch_shapes=exchange_scratch(sems),
         compiler_params=remote(0),
-    )(picks, keys, values)
+    )(vis_blocks.T, vis_count, vis_len.T, keys, values)
     held_1, attn_0, dq_0, slots_0 = pl.pallas_call(
         exchange_and_attend,
         out_shape=(held, half, half, slots),

time: 148 us -> 148 us (level)
  local copies, waits for them, and re-layouts: 8.26 us -> 3.35 us
  Pallas kernels: 136 us -> 140 us
  other arithmetic: 2.45 us -> 4.07 us
    pallas_call x1, Pallas kernels: 44.3 us -> 51.5 us  [body(): pl.pallas_call(return_and_attend, out_shape=(grads, half, half, slots), i...]
    unnamed x20 -> x6, local copies, waits for them, and re-layouts: 8.26 us -> 3.35 us
    pallas_call x2 -> x1, Pallas kernels: 32.1 us -> 27.6 us  [body(): pl.pallas_call(first_exchange, out_shape=(held,) + tuple((shape((n,), jnp...]
    pallas_call x1, Pallas kernels: 28.2 us -> 31.2 us  [body(): pl.pallas_call(exchange_and_attend, out_shape=(held, half, half, slots),...]
    pallas_call x1, Pallas kernels: 31.4 us -> 29.5 us  [body(): pl.pallas_call(last_return, out_shape=(whole, whole), in_specs=[smem] * 2...]
    concatenate x1, other arithmetic: 2.45 us -> 4.07 us  [body(): attention = jnp.concatenate([attn_0, attn_1], axis=1)]
where the time goes in v5:
time: 148 us
  Pallas kernels  140 us (95%)
  other arithmetic  4.07 us (3%)
  local copies, waits for them, and re-layouts  3.35 us (2%)
    pallas_call x1, Pallas kernels, body(): pl.pallas_call(return_and_attend, out_shape=(grads, half, half, slots), i...  51.5 us
    pallas_call x1, Pallas kernels, body(): pl.pallas_call(exchange_and_attend, out_shape=(held, half, half, slots),...  31.2 us
    pallas_call x1, Pallas kernels, body(): pl.pallas_call(last_return, out_shape=(whole, whole), in_specs=[smem] * 2...  29.5 us
    pallas_call x1, Pallas kernels, body(): pl.pallas_call(first_exchange, out_shape=(held,) + tuple((shape((n,), jnp...  27.6 us
    concatenate x1, other arithmetic, body(): attention = jnp.concatenate([attn_0, attn_1], axis=1)  4.07 us
    unnamed x6, local copies, waits for them, and re-layouts  3.35 us

profile of v5, /device:TPU:36, one launch (start us, length us, event | category | flops | bytes accessed | tf_op | source)
XLA Modules:
  0.0 147.9 jit_solution(7452137732241827818)
XLA Ops:
  0.6 27.6 %shard_map.102 = (bf16[40,128,256]{2,1,0:T(8,128)(2,1)}, s32[32]{0:T(128)}, s32[24]{0:T(128)}, s32[24]{0:T(128)}, s32[160]{0:T(256)}) custom-call(s32[6,64]{1,0:T(8,128)} %bitcast.8, s32[64]{0:T(128)} %count_ref.1, s32[6,64]{1,0:T(8,128)} %bitcast.9, bf16[4,128,256]{2,1,0:T(8,128)(2,1)} %bitcast.4, bf16[4,128,256]{2,1,0:T(8,128)(2,1)} %bitcast.6), custom_call_target="tpu_custom_call" | custom-call | tf_op jit(solution)/shard_map/pallas_call | solution.py:669
  28.3 31.2 %shard_map.103 = (bf16[40,128,256]{2,1,0:T(8,128)(2,1)}, bf16[512,1024]{1,0:T(8,128)(2,1)}, bf16[512,1024]{1,0:T(8,128)(2,1)}, bf16[24,128,256]{2,1,0:T(8,128)(2,1)}) custom-call(s32[32]{0:T(128)} %get-tuple-element.19.picks, s32[24]{0:T(128)} %get-tuple-element.20.place, s32[24]{0:T(128)} %get-tuple-element.21.seen, bf16[4,128,256]{2,1,0:T(8,128)(2,1)} %bitcast.5, ...), custom_call_target="tpu_custom_call" | custom-call | tf_op jit(solution)/shard_map/pallas_call | solution.py:677
  59.5 0.0 copy-start
  59.5 0.0 copy-start.1
  59.5 51.5 %shard_map.104 = (bf16[512,256]{1,0:T(8,128)(2,1)}, bf16[512,1024]{1,0:T(8,128)(2,1)}, bf16[512,1024]{1,0:T(8,128)(2,1)}, bf16[24,128,256]{2,1,0:T(8,128)(2,1)}) custom-call(s32[32]{0:T(128)} %get-tuple-element.19.picks, s32[160]{0:T(256)} %get-tuple-element.24.slot_of, s32[24]{0:T(128)} %get-tuple-element.20.place, s32[24]{0:T(128)} %get-tuple-element.21.seen, ...), custom_call_target="tpu_custom_call" | custom-call | tf_op jit(solution)/shard_map/pallas_call | solution.py:685
  111.0 0.0 copy-done
  111.0 0.0 copy-done.1
  111.0 4.1 %pad_maximum_fusion = (bf16[512,2048]{1,0:T(8,128)(2,1)}, bf16[512,2048]{1,0:T(8,128)(2,1)}) fusion(bf16[512,1024]{1,0:T(8,128)(2,1)} %get-tuple-element.27, bf16[512,1024]{1,0:T(8,128)(2,1)S(1)} %copy-done, bf16[512,1024]{1,0:T(8,128)(2,1)} %get-tuple-element.29, bf16[512,1024]{1,0:T(8,128)(2,1)S(1)} %copy-done.1), kind=kLoop, calls=%fused_computation | loop fusion | flops 8388608 | bytes 8388608 | tf_op jit(solution)/shard_map/concatenate | solution.py:701
  115.1 29.5 %shard_map.105 = (bf16[512,256]{1,0:T(8,128)(2,1)}, bf16[512,256]{1,0:T(8,128)(2,1)}) custom-call(s32[32]{0:T(128)} %get-tuple-element.19.picks, s32[160]{0:T(256)} %get-tuple-element.24.slot_of, bf16[24,128,256]{2,1,0:T(8,128)(2,1)} %get-tuple-element.30.done_ref, bf16[512,256]{1,0:T(8,128)(2,1)} %get-tuple-element.31.grads_ref), custom_call_target="tpu_custom_call" | custom-call | tf_op jit(solution)/shard_map/pallas_call | solution.py:693
  144.6 1.7 %copy.13 = bf16[512,256]{1,0:T(8,128)(2,1)} copy(bf16[512,256]{1,0:T(8,128)(2,1)} %get-tuple-element.42) | data formatting | bytes 524288
  146.2 1.7 %copy.14 = bf16[512,256]{1,0:T(8,128)(2,1)} copy(bf16[512,256]{1,0:T(8,128)(2,1)} %get-tuple-element.43) | data formatting | bytes 524288
Async XLA Ops:
  59.5 51.5 %copy-start = (bf16[512,1024]{1,0:T(8,128)(2,1)S(1)}, bf16[512,1024]{1,0:T(8,128)(2,1)}, u32[]{:S(2)}) copy-start(bf16[512,1024]{1,0:T(8,128)(2,1)} %get-tuple-element.23) | copy-start | bytes 3145732
  59.5 51.5 %copy-start.1 = (bf16[512,1024]{1,0:T(8,128)(2,1)S(1)}, bf16[512,1024]{1,0:T(8,128)(2,1)}, u32[]{:S(2)}) copy-start(bf16[512,1024]{1,0:T(8,128)(2,1)} %get-tuple-element.28) | copy-start | bytes 3145732

commit v6 on v5

--- a/solution.py
+++ b/solution.py
@@ -56,6 +56,11 @@
 def nth(n, z):
     d = (n + 1) // 2
     return z + jnp.where(lax.rem(n, 2) == 1, -d, d), d
+
+
+def target(j, z):
+    inner = jnp.where(j == 0, 3, jnp.where(j == 1, 0, jnp.where(j == 2, 2, 1)))
+    return jnp.where(z == 0, 3 - j, jnp.where(z == 3, j, jnp.where(z == 1, inner, 3 - inner)))
 
 
 def chosen(blocks_ref, count_ref, dst, src):
@@ -491,28 +496,22 @@
             device_id_type=MESH,
         )
 
-    def inside(zs):
-        return (zs >= 0) & (zs < SIDE)
-
-    @pl.loop(0, STEPS)
-    def _(n):
-        zs, _ = nth(STEPS - 1 - n, z)
-
-        @pl.when(inside(zs))
-        def _():
-            @pl.loop(0, y)
-            def _(h):
-                hop = jnp.where(y == 1, 1, jnp.where(h == 0, 2, jnp.where(h == 1, 1, 3)))
-                ys = y - hop
-                for c in range(CAP):
-                    far[ys * SIDE + zs, c] = gathered(ROW + (ys * SIDE + zs) * CAP + c).astype(far.dtype)
-                pl.when(hop == 2)(lambda: y_far(ys, zs).start())
-                pl.when(hop != 2)(lambda: y_near(ys, zs).start())
-
-    def relay_step(n):
-        zs, _ = nth(n, z)
-
-        @pl.when(inside(zs) & (y >= 2))
+    def send(j):
+        zs = target(j, z)
+
+        @pl.loop(0, y)
+        def _(h):
+            hop = jnp.where(y == 1, 1, jnp.where(h == 0, 2, jnp.where(h == 1, 1, 3)))
+            ys = y - hop
+            for c in range(CAP):
+                far[ys * SIDE + zs, c] = gathered(ROW + (ys * SIDE + zs) * CAP + c).astype(far.dtype)
+            pl.when(hop == 2)(lambda: y_far(ys, zs).start())
+            pl.when(hop != 2)(lambda: y_near(ys, zs).start())
+
+    def pass_on(j):
+        zs = target(j, z)
+
+        @pl.when(y >= 2)
         def _():
             pltpu.make_async_remote_copy(
                 src_ref=relay.at[zs],
@@ -524,10 +523,10 @@
             ).wait_recv()
             relay_copy(zs).start()
 
-    def step(n):
-        zs, d = nth(n, z)
-
-        @pl.when(inside(zs) & ((zs <= z) | (y < SIDE - 1)))
+    def add_up(j):
+        zs = target(j, z)
+
+        @pl.when((zs <= z) | (y < SIDE - 1))
         def _():
             for t in range(PER):
                 total[t] = gathered(zs * PER + t)
@@ -562,32 +561,29 @@
                     z_copy(zs, half, z, from_left, left_recv).wait_recv()
                     total[blocks] += from_left[zs, blocks].astype(jnp.float32)
 
-                @pl.when(d > 0)
+                @pl.when(zs != z)
                 def _():
                     running[zs, blocks] = total[blocks].astype(running.dtype)
                     pl.when(zs < z)(lambda: z_copy(zs, half, z - 1, from_right, right_recv).start())
                     pl.when(zs > z)(lambda: z_copy(zs, half, z + 1, from_left, left_recv).start())
 
-    def relay_nth(n):
-        relay_step(STEPS - 1 - n)
-
-    def step_nth(n):
-        step(STEPS - 1 - n)
-
+    send(jnp.int32(0))
     if attention:
         attention.wait()
 
         def between(k):
-            pl.loop(*listed(k, {2: (0, 2), 4: (2, 4), 6: (4, 6), 8: (6, 7)}))(step_nth)
-            pl.loop(*listed(k, {1: (0, 2), 2: (2, 4), 4: (4, 6), 6: (6, 7)}))(relay_nth)
+            pl.loop(*listed(k, {1: (0, 1), 4: (1, 2), 6: (2, 3), 8: (3, 4)}))(pass_on)
+            pl.loop(*listed(k, {1: (1, 2), 3: (2, 3), 5: (3, 4)}))(send)
+            pl.loop(*listed(k, {3: (0, 1), 6: (1, 2), 8: (2, 3), 10: (3, 4)}))(add_up)
 
         attention.run(between)
     else:
 
-        @pl.loop(0, STEPS)
-        def _(n):
-            relay_nth(n)
-            step_nth(n)
+        @pl.loop(0, SIDE)
+        def _(j):
+            pass_on(j)
+            pl.when(j < SIDE - 1)(lambda: send(j + 1))
+            add_up(j)
 
     write(total)
 
@@ -659,8 +655,8 @@
     grads = shape((tokens, 2 * D), bf16)
     whole = shape((tokens, width), bf16)
 
-    def remote(n):
-        return pltpu.CompilerParams(collective_id=n, has_side_effects=True, vmem_limit_bytes=56 * MIB)
+    def remote(n, mib):
+        return pltpu.CompilerParams(collective_id=n, has_side_effects=True, vmem_limit_bytes=mib * MIB)
 
     keys = key_states.reshape(PER, BLOCK, width)
     values = value_state_rows.reshape(PER, BLOCK, width)
@@ -672,7 +668,7 @@
         in_specs=[smem] * 3 + [hbm] * 2,
         out_specs=(hbm,) + (smem,) * 4,
         scratch_shapes=exchange_scratch(sems),
-        compiler_params=remote(0),
+        compiler_params=remote(0, 58),
     )(vis_blocks.T, vis_count, vis_len.T, keys, values)
     held_1, attn_0, dq_0, slots_0 = pl.pallas_call(
         exchange_and_attend,
@@ -680,7 +676,7 @@
         in_specs=[smem] * 3 + [hbm] * 5,
         out_specs=(hbm, vmem, vmem, vmem),
         scratch_shapes=Attention.scratch(tokens, lanes) + exchange_scratch(sems),
-        compiler_params=remote(1),
+        compiler_params=remote(1, 58),
     )(picks, place, seen, keys, values, query_states, grad_out, held_0)
     grads_0, attn_1, dq_1, slots_1 = pl.pallas_call(
         return_and_attend,
@@ -688,7 +684,7 @@
         in_specs=[smem] * 4 + [hbm] * 3 + [vmem],
         out_specs=(vmem, vmem, vmem, vmem),
         scratch_shapes=Attention.scratch(tokens, lanes) + return_scratch(sems),
-        compiler_params=remote(2),
+        compiler_params=remote(2, 48),
     )(picks, slot_of, place, seen, query_states, grad_out, held_1, slots_0)
     grad_key, grad_value = pl.pallas_call(
         last_return,
@@ -696,7 +692,7 @@
         in_specs=[smem] * 2 + [vmem] * 2,
         out_specs=(vmem, vmem),
         scratch_shapes=return_scratch(sems),
-        compiler_params=remote(3),
+        compiler_params=remote(3, 24),
     )(picks, slot_of, slots_1, grads_0)
     attention = jnp.concatenate([attn_0, attn_1], axis=1)
     grad_query = jnp.concatenate([dq_0, dq_1], axis=1)

time: 148 us -> 139 us (0.939)
  Pallas kernels: 140 us -> 132 us
  other arithmetic: 4.07 us -> 2.45 us
    pallas_call x1, Pallas kernels: 51.5 us -> 43.3 us  [body(): pl.pallas_call(return_and_attend, out_shape=(grads, half, half, slots), i...]
    concatenate x1, other arithmetic: 4.07 us -> 2.45 us  [body(): attention = jnp.concatenate([attn_0, attn_1], axis=1)]
    unnamed x6 -> x16, local copies, waits for them, and re-layouts: 3.35 us -> 2.83 us
where the time goes in v6:
time: 139 us; the launch traced here: 138 us
  Pallas kernels  132 us (95%)
  local copies, waits for them, and re-layouts  2.83 us (2%)
  other arithmetic  2.45 us (2%)
    pallas_call x1, Pallas kernels, body(): pl.pallas_call(return_and_attend, out_shape=(grads, half, half, slots), i...  43.3 us
    pallas_call x1, Pallas kernels, body(): pl.pallas_call(exchange_and_attend, out_shape=(held, half, half, slots),...  31.1 us
    pallas_call x1, Pallas kernels, body(): pl.pallas_call(last_return, out_shape=(whole, whole), in_specs=[smem] * 2...  30.3 us
    pallas_call x1, Pallas kernels, body(): pl.pallas_call(first_exchange, out_shape=(held,) + tuple((shape((n,), jnp...  27.6 us
    unnamed x16, local copies, waits for them, and re-layouts  2.83 us

profile of v6, /device:TPU:36, one launch (start us, length us, event | category | flops | bytes accessed | tf_op | source)
XLA Modules:
  0.0 138.4 jit_solution(705096958564781451)
XLA Ops:
  0.6 27.6 %shard_map.102 = (bf16[40,128,256]{2,1,0:T(8,128)(2,1)}, s32[32]{0:T(128)}, s32[24]{0:T(128)}, s32[24]{0:T(128)}, s32[160]{0:T(256)}) custom-call(s32[6,64]{1,0:T(8,128)} %bitcast.8, s32[64]{0:T(128)} %count_ref.1, s32[6,64]{1,0:T(8,128)} %bitcast.9, bf16[4,128,256]{2,1,0:T(8,128)(2,1)} %bitcast.4, bf16[4,128,256]{2,1,0:T(8,128)(2,1)} %bitcast.6), custom_call_target="tpu_custom_call" | custom-call | tf_op jit(solution)/shard_map/pallas_call | solution.py:665
  28.3 0.0 copy-start.1
  28.3 0.0 copy-start.2
  28.3 0.0 copy-start.3
  28.3 0.0 copy-start.4
  28.3 31.1 %shard_map.103 = (bf16[40,128,256]{2,1,0:T(8,128)(2,1)}, bf16[512,1024]{1,0:T(8,128)(2,1)}, bf16[512,1024]{1,0:T(8,128)(2,1)}, bf16[24,128,256]{2,1,0:T(8,128)(2,1)}) custom-call(s32[32]{0:T(128)} %get-tuple-element.19.picks, s32[24]{0:T(128)} %get-tuple-element.20.place, s32[24]{0:T(128)} %get-tuple-element.21.seen, bf16[4,128,256]{2,1,0:T(8,128)(2,1)} %bitcast.5, ...), custom_call_target="tpu_custom_call" | custom-call | tf_op jit(solution)/shard_map/pallas_call | solution.py:673
  59.5 0.0 copy-done.1
  59.5 0.0 copy-done.2
  59.5 0.0 copy-done.3
  59.5 0.0 copy-done.4
  59.5 0.0 copy-start
  59.5 1.4 %copy-done = bf16[24,128,256]{2,1,0:T(8,128)(2,1)S(1)} copy-done((bf16[24,128,256]{2,1,0:T(8,128)(2,1)S(1)}, bf16[24,128,256]{2,1,0:T(8,128)(2,1)}, u32[]{:S(2)}) %copy-start) | copy-done | bytes 1572888
  60.9 0.0 copy-start.5
  60.9 0.0 copy-start.6
  60.9 43.3 %shard_map.104 = (bf16[512,256]{1,0:T(8,128)(2,1)S(1)}, bf16[512,1024]{1,0:T(8,128)(2,1)S(1)}, bf16[512,1024]{1,0:T(8,128)(2,1)S(1)}, bf16[24,128,256]{2,1,0:T(8,128)(2,1)S(1)}) custom-call(s32[32]{0:T(128)S(1)} %copy-done.1, s32[160]{0:T(256)S(1)} %copy-done.2, s32[24]{0:T(128)S(1)} %copy-done.3, s32[24]{0:T(128)S(1)} %copy-done.4, ...), custom_call_target="tpu_custom_call" | custom-call | tf_op jit(solution)/shard_map/pallas_call | solution.py:681
  104.2 0.0 copy-done.5
  104.2 0.0 copy-done.6
  104.2 2.5 %pad_maximum_fusion = (bf16[512,2048]{1,0:T(8,128)(2,1)}, bf16[512,2048]{1,0:T(8,128)(2,1)}) fusion(bf16[512,1024]{1,0:T(8,128)(2,1)S(1)} %get-tuple-element.27, bf16[512,1024]{1,0:T(8,128)(2,1)S(1)} %copy-done.5, bf16[512,1024]{1,0:T(8,128)(2,1)S(1)} %get-tuple-element.29, bf16[512,1024]{1,0:T(8,128)(2,1)S(1)} %copy-done.6), kind=kLoop, calls=%fused_computation | loop fusion | flops 8388608 | bytes 8388608 | tf_op jit(solution)/shard_map/concatenate | solution.py:697
  106.7 30.3 %shard_map.105 = (bf16[512,256]{1,0:T(8,128)(2,1)S(1)}, bf16[512,256]{1,0:T(8,128)(2,1)S(1)}) custom-call(s32[32]{0:T(128)S(1)} %copy-done.1, s32[160]{0:T(256)S(1)} %copy-done.2, bf16[24,128,256]{2,1,0:T(8,128)(2,1)S(1)} %get-tuple-element.30.done_ref, bf16[512,256]{1,0:T(8,128)(2,1)S(1)} %get-tuple-element.31.grads_ref), custom_call_target="tpu_custom_call" | custom-call | tf_op jit(solution)/shard_map/pallas_call | solution.py:689
  137.0 0.7 copy.13
  137.7 0.7 copy.14
Async XLA Ops:
  28.3 31.2 %copy-start.1 = (s32[32]{0:T(128)S(1)}, s32[32]{0:T(128)}, u32[]{:S(2)}) copy-start(s32[32]{0:T(128)} %get-tuple-element.19.picks) | copy-start | bytes 388
  28.3 31.2 %copy-start.2 = (s32[160]{0:T(256)S(1)}, s32[160]{0:T(256)}, u32[]{:S(2)}) copy-start(s32[160]{0:T(256)} %get-tuple-element.24.slot_of) | copy-start | bytes 1924
  28.3 31.2 %copy-start.3 = (s32[24]{0:T(128)S(1)}, s32[24]{0:T(128)}, u32[]{:S(2)}) copy-start(s32[24]{0:T(128)} %get-tuple-element.20.place) | copy-start | bytes 292
  28.3 31.2 %copy-start.4 = (s32[24]{0:T(128)S(1)}, s32[24]{0:T(128)}, u32[]{:S(2)}) copy-start(s32[24]{0:T(128)} %get-tuple-element.21.seen) | copy-start | bytes 292
  59.5 1.4 %copy-start = (bf16[24,128,256]{2,1,0:T(8,128)(2,1)S(1)}, bf16[24,128,256]{2,1,0:T(8,128)(2,1)}, u32[]{:S(2)}) copy-start(bf16[24,128,256]{2,1,0:T(8,128)(2,1)} %get-tuple-element.26.done_ref) | copy-start | bytes 4718596
  60.9 43.3 %copy-start.5 = (bf16[512,1024]{1,0:T(8,128)(2,1)S(1)}, bf16[512,1024]{1,0:T(8,128)(2,1)}, u32[]{:S(2)}) copy-start(bf16[512,1024]{1,0:T(8,128)(2,1)} %get-tuple-element.23) | copy-start | bytes 3145732
  60.9 43.3 %copy-start.6 = (bf16[512,1024]{1,0:T(8,128)(2,1)S(1)}, bf16[512,1024]{1,0:T(8,128)(2,1)}, u32[]{:S(2)}) copy-start(bf16[512,1024]{1,0:T(8,128)(2,1)} %get-tuple-element.28) | copy-start | bytes 3145732

commit v7 on v6

--- a/solution.py
+++ b/solution.py
@@ -143,12 +143,19 @@
         ]
 
     def start(self):
-        for load in self.loads:
+        for load in self.loads[:2]:
             load.start()
 
-    def wait(self):
+    def load_held(self):
+        self.loads[2].start()
+
+    def wait_all(self):
         for load in self.loads:
             load.wait()
+
+    def wait(self):
+        self.load_held()
+        self.wait_all()
 
     def weigh(self, i):
         f32, bf16 = jnp.float32, jnp.bfloat16
@@ -257,7 +264,12 @@
     ]
 
 
-def exchange(head, picks_ref, k_ref, v_ref, out_ref, scratch, attention, lists=None):
+class Steps:
+    def __init__(self, **steps):
+        self.__dict__.update(steps)
+
+
+def exchange(head, picks_ref, k_ref, v_ref, out_ref, scratch, lists):
     row, packed, relay, z_recv, up_send, down_send, far_recv, y_send, relay_recv, relay_send, keep_sem, in_sem = scratch
     me, y, z = coords()
     columns = pl.ds(head * D, D)
@@ -265,13 +277,14 @@
         pltpu.make_async_copy(k_ref.at[:, :, columns], row.at[z, :, :, pl.ds(0, D)], in_sem.at[0]),
         pltpu.make_async_copy(v_ref.at[:, :, columns], row.at[z, :, :, pl.ds(D, D)], in_sem.at[1]),
     )
-    for copy in mine_in:
-        copy.start()
-    if attention:
-        attention.start()
-    barrier_neighbours(y, z)
-    for copy in mine_in:
-        copy.wait()
+
+    def load():
+        for copy in mine_in:
+            copy.start()
+
+    def loaded():
+        for copy in mine_in:
+            copy.wait()
 
     def z_copy(zs, to, sems):
         return pltpu.make_async_remote_copy(
@@ -372,51 +385,44 @@
             ).wait_recv()
             relay_copy(zs).start()
 
-    step(jnp.int32(0))
-    if attention:
-        attention.wait()
-
-        def between(k):
-            pl.loop(*listed(k, {1: (1, 3), 4: (3, 5), 7: (5, 7)}))(step)
-            pl.loop(*listed(k, {1: (0, 1), 4: (1, 3), 7: (3, 5), 9: (5, 7)}))(relay_step)
-
-        attention.run(between)
-    else:
-        tables(*lists)
-
-        @pl.loop(1, STEPS + 1)
+    def arrived():
+        @pl.loop(0, y * SIDE)
         def _(n):
-            pl.when(n < STEPS)(lambda: step(n))
-            relay_step(n - 1)
-
-    @pl.loop(0, y * SIDE)
-    def _(n):
-        pltpu.make_async_remote_copy(
-            src_ref=packed.at[0, 0],
-            dst_ref=out_ref.at[pl.ds(ROW + n * CAP, CAP)],
-            send_sem=relay_send.at[0],
-            recv_sem=far_recv.at[n],
-            device_id=at(y, z),
-            device_id_type=MESH,
-        ).wait_recv()
-
-    @pl.loop(0, SIDE)
-    def _(zs):
-        _, mine = wanted(zs)
-
-        @pl.when(mine)
-        def _():
-            pl.when((zs <= z) & (z < SIDE - 1))(lambda: z_copy(zs, z + 1, up_send).wait_send())
-            pl.when((zs >= z) & (z > 0) & (y < SIDE - 1))(
-                lambda: z_copy(zs, z - 1, down_send).wait_send()
-            )
-            keep(zs).wait()
-
-        @pl.loop(y + 1, SIDE)
-        def _(yd):
-            y_near(yd, zs).wait_send()
-
-        pl.when(y >= 2)(lambda: relay_copy(zs).wait_send())
+            pltpu.make_async_remote_copy(
+                src_ref=packed.at[0, 0],
+                dst_ref=out_ref.at[pl.ds(ROW + n * CAP, CAP)],
+                send_sem=relay_send.at[0],
+                recv_sem=far_recv.at[n],
+                device_id=at(y, z),
+                device_id_type=MESH,
+            ).wait_recv()
+
+        @pl.loop(0, SIDE)
+        def _(zs):
+            _, mine = wanted(zs)
+            pl.when(mine)(lambda: keep(zs).wait())
+
+    def sent():
+        @pl.loop(0, SIDE)
+        def _(zs):
+            _, mine = wanted(zs)
+
+            @pl.when(mine)
+            def _():
+                pl.when((zs <= z) & (z < SIDE - 1))(
+                    lambda: z_copy(zs, z + 1, up_send).wait_send()
+                )
+                pl.when((zs >= z) & (z > 0) & (y < SIDE - 1))(
+                    lambda: z_copy(zs, z - 1, down_send).wait_send()
+                )
+
+            @pl.loop(y + 1, SIDE)
+            def _(yd):
+                y_near(yd, zs).wait_send()
+
+            pl.when(y >= 2)(lambda: relay_copy(zs).wait_send())
+
+    return Steps(load=load, loaded=loaded, step=step, relay=relay_step, arrived=arrived, sent=sent)
 
 
 def return_scratch(sems):
@@ -439,13 +445,10 @@
     ]
 
 
-def give_back(picks_ref, slot_of, slots_ref, write, scratch, attention):
+def give_back(picks_ref, slot_of, slots_ref, scratch):
     (far, landed, relay, running, from_left, from_right, total,
      y_send, y_recv, relay_send, relay_recv, z_send, left_recv, right_recv) = scratch
     me, y, z = coords()
-    if attention:
-        attention.start()
-    barrier_neighbours(y, z)
 
     def gathered(e):
         out = jnp.zeros((BLOCK, 2 * D), jnp.float32)
@@ -567,76 +570,108 @@
                     pl.when(zs < z)(lambda: z_copy(zs, half, z - 1, from_right, right_recv).start())
                     pl.when(zs > z)(lambda: z_copy(zs, half, z + 1, from_left, left_recv).start())
 
-    send(jnp.int32(0))
-    if attention:
-        attention.wait()
-
-        def between(k):
-            pl.loop(*listed(k, {1: (0, 1), 4: (1, 2), 6: (2, 3), 8: (3, 4)}))(pass_on)
-            pl.loop(*listed(k, {1: (1, 2), 3: (2, 3), 5: (3, 4)}))(send)
-            pl.loop(*listed(k, {3: (0, 1), 6: (1, 2), 8: (2, 3), 10: (3, 4)}))(add_up)
-
-        attention.run(between)
-    else:
-
+    def sent():
         @pl.loop(0, SIDE)
-        def _(j):
-            pass_on(j)
-            pl.when(j < SIDE - 1)(lambda: send(j + 1))
-            add_up(j)
-
-    write(total)
+        def _(zs):
+            @pl.when((zs < z) | ((zs > z) & (y < SIDE - 1)))
+            def _():
+                for half in range(2):
+                    z_copy(zs, half, z, from_right, right_recv).wait_send()
+
+            @pl.loop(0, y)
+            def _(ys):
+                y_near(ys, zs).wait_send()
+
+            pl.when(y >= 2)(lambda: relay_copy(zs).wait_send())
+
+    return Steps(send=send, pass_on=pass_on, add_up=add_up, sent=sent, total=total)
+
+
+N_ATTEND, N_EXCHANGE, N_RETURN = 13, 12, 14
+
+
+def gather_and_attend(
+    blocks_ref, count_ref, len_ref, k_ref, v_ref, q_ref, do_ref,
+    held_0, held_1, picks, place, seen, slot_of, attn_ref, dq_ref, slots_ref, *scratch,
+):
+    _, y, z = coords()
+    lists = (blocks_ref, count_ref, len_ref, place, seen, slot_of)
+    attention = Attention(0, place, seen, q_ref, do_ref, held_0, attn_ref, dq_ref, slots_ref, scratch[:N_ATTEND])
+    scratch = scratch[N_ATTEND:]
+    first = exchange(0, picks, k_ref, v_ref, held_0, scratch[:N_EXCHANGE], lists)
+    second = exchange(1, picks, k_ref, v_ref, held_1, scratch[N_EXCHANGE:], None)
+    first.load()
+    second.load()
+    attention.start()
+    barrier_neighbours(y, z)
+    first.loaded()
+    first.step(jnp.int32(0))
+    tables(*lists)
+    second.loaded()
+
+    @pl.loop(1, STEPS)
+    def _(n):
+        first.step(n)
+        first.relay(n - 1)
+
+    second.step(jnp.int32(0))
+    first.relay(jnp.int32(STEPS - 1))
+
+    @pl.loop(1, 3)
+    def _(n):
+        second.step(n)
+        second.relay(n - 1)
+
+    first.arrived()
+    attention.wait()
+
+    def between(k):
+        pl.loop(*listed(k, {0: (3, 5), 4: (5, 7)}))(second.step)
+        pl.loop(*listed(k, {0: (2, 3), 2: (3, 5), 7: (5, 7)}))(second.relay)
+
+    attention.run(between)
+    second.arrived()
+    first.sent()
+    second.sent()
+
+
+def attend_and_return(
+    picks, slot_of, place, seen, q_ref, do_ref, held_ref, done_ref,
+    gk_ref, gv_ref, attn_ref, dq_ref, slots_ref, *scratch,
+):
+    _, y, z = coords()
+    attention = Attention(1, place, seen, q_ref, do_ref, held_ref, attn_ref, dq_ref, slots_ref, scratch[:N_ATTEND])
+    scratch = scratch[N_ATTEND:]
+    first = give_back(picks, slot_of, done_ref, scratch[:N_RETURN])
+    second = give_back(picks, slot_of, slots_ref, scratch[N_RETURN:])
+    attention.start()
+    attention.load_held()
+    barrier_neighbours(y, z)
+    first.send(jnp.int32(0))
+    attention.wait_all()
+
+    def between(k):
+        pl.loop(*listed(k, {4: (0, 1), 7: (1, 2), 10: (2, 3)}))(first.add_up)
+        pl.loop(*listed(k, {1: (0, 1), 4: (1, 2), 7: (2, 3), 10: (3, 4)}))(first.pass_on)
+        pl.loop(*listed(k, {1: (1, 2), 4: (2, 3), 7: (3, 4)}))(first.send)
+
+    attention.run(between)
+    second.send(jnp.int32(0))
+    first.add_up(jnp.int32(SIDE - 1))
 
     @pl.loop(0, SIDE)
-    def _(zs):
-        @pl.when((zs < z) | ((zs > z) & (y < SIDE - 1)))
-        def _():
-            for half in range(2):
-                z_copy(zs, half, z, from_right, right_recv).wait_send()
-
-        @pl.loop(0, y)
-        def _(ys):
-            y_near(ys, zs).wait_send()
-
-        pl.when(y >= 2)(lambda: relay_copy(zs).wait_send())
-
-
-def first_exchange(
-    blocks_ref, count_ref, len_ref, k_ref, v_ref, held_ref, picks, place, seen, slot_of, *scratch
-):
-    lists = (blocks_ref, count_ref, len_ref, place, seen, slot_of)
-    exchange(0, picks, k_ref, v_ref, held_ref, scratch, None, lists)
-
-
-def exchange_and_attend(
-    picks, place, seen, k_ref, v_ref, q_ref, do_ref, held_ref, next_ref, attn_ref, dq_ref, slots_ref, *scratch
-):
-    attention = Attention(0, place, seen, q_ref, do_ref, held_ref, attn_ref, dq_ref, slots_ref, scratch[:13])
-    exchange(1, picks, k_ref, v_ref, next_ref, scratch[13:], attention)
-
-
-def return_and_attend(
-    picks, slot_of, place, seen, q_ref, do_ref, held_ref, done_ref, grads_ref, attn_ref, dq_ref, slots_ref, *scratch
-):
-    attention = Attention(1, place, seen, q_ref, do_ref, held_ref, attn_ref, dq_ref, slots_ref, scratch[:13])
-
-    def write(total):
-        for t in range(PER):
-            grads_ref[pl.ds(t * BLOCK, BLOCK), :] = total[t].astype(grads_ref.dtype)
-
-    give_back(picks, slot_of, done_ref, write, scratch[13:], attention)
-
-
-def last_return(picks, slot_of, done_ref, grads_ref, gk_ref, gv_ref, *scratch):
-    def write(total):
-        gk_ref[:, :D] = grads_ref[:, :D]
-        gv_ref[:, :D] = grads_ref[:, D:]
+    def _(j):
+        second.pass_on(j)
+        pl.when(j < SIDE - 1)(lambda: second.send(j + 1))
+        second.add_up(j)
+
+    for part, lanes in ((first, slice(0, D)), (second, slice(D, 2 * D))):
         for t in range(PER):
             rows = pl.ds(t * BLOCK, BLOCK)
-            gk_ref[rows, D:] = total[t, :, :D].astype(gk_ref.dtype)
-            gv_ref[rows, D:] = total[t, :, D:].astype(gv_ref.dtype)
-
-    give_back(picks, slot_of, done_ref, write, scratch, None)
+            gk_ref[rows, lanes] = part.total[t, :, :D].astype(gk_ref.dtype)
+            gv_ref[rows, lanes] = part.total[t, :, D:].astype(gv_ref.dtype)
+    first.sent()
+    second.sent()
 
 
 def body(query_states, key_states, value_state_rows, grad_out, vis_blocks, vis_count, vis_len):
@@ -652,7 +687,6 @@
     held = shape((HELD, BLOCK, 2 * D), bf16)
     half = shape((tokens, lanes), bf16)
     slots = shape((PER * VIS, BLOCK, 2 * D), bf16)
-    grads = shape((tokens, 2 * D), bf16)
     whole = shape((tokens, width), bf16)
 
     def remote(n, mib):
@@ -662,38 +696,22 @@
     values = value_state_rows.reshape(PER, BLOCK, width)
 
     sizes = (CTX * CAP, PER * VIS, PER * VIS, PER * HELD)
-    held_0, picks, place, seen, slot_of = pl.pallas_call(
-        first_exchange,
-        out_shape=(held,) + tuple(shape((n,), jnp.int32) for n in sizes),
-        in_specs=[smem] * 3 + [hbm] * 2,
-        out_specs=(hbm,) + (smem,) * 4,
-        scratch_shapes=exchange_scratch(sems),
+    _, held_1, picks, place, seen, slot_of, attn_0, dq_0, slots_0 = pl.pallas_call(
+        gather_and_attend,
+        out_shape=(held, held) + tuple(shape((n,), jnp.int32) for n in sizes) + (half, half, slots),
+        in_specs=[smem] * 3 + [hbm] * 4,
+        out_specs=(hbm,) * 2 + (smem,) * 4 + (vmem,) * 3,
+        scratch_shapes=Attention.scratch(tokens, lanes) + 2 * exchange_scratch(sems),
         compiler_params=remote(0, 58),
-    )(vis_blocks.T, vis_count, vis_len.T, keys, values)
-    held_1, attn_0, dq_0, slots_0 = pl.pallas_call(
-        exchange_and_attend,
-        out_shape=(held, half, half, slots),
-        in_specs=[smem] * 3 + [hbm] * 5,
-        out_specs=(hbm, vmem, vmem, vmem),
-        scratch_shapes=Attention.scratch(tokens, lanes) + exchange_scratch(sems),
-        compiler_params=remote(1, 58),
-    )(picks, place, seen, keys, values, query_states, grad_out, held_0)
-    grads_0, attn_1, dq_1, slots_1 = pl.pallas_call(
-        return_and_attend,
-        out_shape=(grads, half, half, slots),
+    )(vis_blocks.T, vis_count, vis_len.T, keys, values, query_states, grad_out)
+    grad_key, grad_value, attn_1, dq_1, _ = pl.pallas_call(
+        attend_and_return,
+        out_shape=(whole, whole, half, half, slots),
         in_specs=[smem] * 4 + [hbm] * 3 + [vmem],
-        out_specs=(vmem, vmem, vmem, vmem),
-        scratch_shapes=Attention.scratch(tokens, lanes) + return_scratch(sems),
-        compiler_params=remote(2, 48),
+        out_specs=(vmem,) * 5,
+        scratch_shapes=Attention.scratch(tokens, lanes) + 2 * return_scratch(sems),
+        compiler_params=remote(1, 48),
     )(picks, slot_of, place, seen, query_states, grad_out, held_1, slots_0)
-    grad_key, grad_value = pl.pallas_call(
-        last_return,
-        out_shape=(whole, whole),
-        in_specs=[smem] * 2 + [vmem] * 2,
-        out_specs=(vmem, vmem),
-        scratch_shapes=return_scratch(sems),
-        compiler_params=remote(3, 24),
-    )(picks, slot_of, slots_1, grads_0)
     attention = jnp.concatenate([attn_0, attn_1], axis=1)
     grad_query = jnp.concatenate([dq_0, dq_1], axis=1)
     return attention, grad_query, grad_key, grad_value

time: 139 us -> 130 us (0.935)
  Pallas kernels: 132 us -> 121 us
  local copies, waits for them, and re-layouts: 2.83 us -> 5.44 us
    pallas_call x4 -> x2, Pallas kernels: 132 us -> 121 us  [the longest x1 67.7 us: body(): pl.pallas_call(attend_and_return, out_shape=(whole, whole, half, half, sl...]
    unnamed x16, local copies, waits for them, and re-layouts: 2.83 us -> 5.44 us
where the time goes in v7:
time: 130 us
  Pallas kernels  121 us (93%)
  local copies, waits for them, and re-layouts  5.44 us (4%)
  other arithmetic  2.45 us (2%)
    pallas_call x1, Pallas kernels, body(): pl.pallas_call(attend_and_return, out_shape=(whole, whole, half, half, sl...  67.7 us
    pallas_call x1, Pallas kernels, body(): pl.pallas_call(gather_and_attend, out_shape=(held, held) + tuple((shape((...  53.7 us
    unnamed x16, local copies, waits for them, and re-layouts  5.44 us

profile of v7, /device:TPU:36, one launch (start us, length us, event | category | flops | bytes accessed | tf_op | source)
XLA Modules:
  0.0 130.0 jit_solution(17202623705760791581)
XLA Ops:
  0.6 53.7 %shard_map.102 = (bf16[40,128,256]{2,1,0:T(8,128)(2,1)}, bf16[40,128,256]{2,1,0:T(8,128)(2,1)}, s32[32]{0:T(128)}, s32[24]{0:T(128)}, s32[24]{0:T(128)}, /*index...) custom-call(s32[6,64]{1,0:T(8,128)} %bitcast.6, s32[64]{0:T(128)} %count_ref.1, ...), custom_call_target="tpu_custom_call" | custom-call | tf_op jit(solution)/shard_map/pallas_call | solution.py:699
  54.4 0.0 copy-start
  54.4 1.4 %copy-done = bf16[24,128,256]{2,1,0:T(8,128)(2,1)S(1)} copy-done((bf16[24,128,256]{2,1,0:T(8,128)(2,1)S(1)}, bf16[24,128,256]{2,1,0:T(8,128)(2,1)}, u32[]{:S(2)}) %copy-start) | copy-done | bytes 1572888
  55.8 0.0 copy-start.1
  55.8 0.7 copy-done.1
  56.5 0.0 copy-start.2
  56.5 0.7 copy-done.2
  57.1 0.0 copy-start.3
  57.1 0.7 copy-done.3
  57.8 0.0 copy-start.4
  57.8 0.6 copy-done.4
  58.4 0.0 copy-start.5
  58.4 0.0 copy-start.6
  58.4 67.7 %shard_map.103 = (bf16[512,256]{1,0:T(8,128)(2,1)S(1)}, bf16[512,256]{1,0:T(8,128)(2,1)S(1)}, bf16[512,1024]{1,0:T(8,128)(2,1)S(1)}, bf16[512,1024]{1,0:T(8,128)(2,1)S(1)}, bf16[24,128,256]{2,1,0:T(8,128)(2,1)}) custom-call(s32[32]{0:T(128)S(1)} %copy-done.2, s32[160]{0:T(256)S(1)} %copy-done.1, s32[24]{0:T(128)S(1)} %copy-done.3, s32[24]{0:T(128)S(1)} %copy-done.4, ...), custom_call_target="tpu_custom_call" | custom-call | tf_op jit(solution)/shard_map/pallas_call | solution.py:707
  126.1 0.0 copy-done.5
  126.1 0.0 copy-done.6
  126.1 2.5 %pad_maximum_fusion = (bf16[512,2048]{1,0:T(8,128)(2,1)}, bf16[512,2048]{1,0:T(8,128)(2,1)}) fusion(bf16[512,1024]{1,0:T(8,128)(2,1)S(1)} %get-tuple-element.23, bf16[512,1024]{1,0:T(8,128)(2,1)S(1)} %copy-done.5, bf16[512,1024]{1,0:T(8,128)(2,1)S(1)} %get-tuple-element.25, bf16[512,1024]{1,0:T(8,128)(2,1)S(1)} %copy-done.6), kind=kLoop, calls=%fused_computation | loop fusion | flops 8388608 | bytes 8388608 | tf_op jit(solution)/shard_map/concatenate | solution.py:715
  128.6 0.7 copy.13
  129.3 0.7 copy.14
Async XLA Ops:
  54.4 1.4 %copy-start = (bf16[24,128,256]{2,1,0:T(8,128)(2,1)S(1)}, bf16[24,128,256]{2,1,0:T(8,128)(2,1)}, u32[]{:S(2)}) copy-start(bf16[24,128,256]{2,1,0:T(8,128)(2,1)} %get-tuple-element.22.done_ref) | copy-start | bytes 4718596
  55.8 0.7 copy-start.1
  56.5 0.7 copy-start.2
  57.1 0.7 copy-start.3
  57.8 0.6 copy-start.4
  58.4 67.7 %copy-start.5 = (bf16[512,1024]{1,0:T(8,128)(2,1)S(1)}, bf16[512,1024]{1,0:T(8,128)(2,1)}, u32[]{:S(2)}) copy-start(bf16[512,1024]{1,0:T(8,128)(2,1)} %get-tuple-element.16) | copy-start | bytes 3145732
  58.4 67.7 %copy-start.6 = (bf16[512,1024]{1,0:T(8,128)(2,1)S(1)}, bf16[512,1024]{1,0:T(8,128)(2,1)}, u32[]{:S(2)}) copy-start(bf16[512,1024]{1,0:T(8,128)(2,1)} %get-tuple-element.24) | copy-start | bytes 3145732

commit v8 on v7

--- a/solution.py
+++ b/solution.py
@@ -61,6 +61,22 @@
 def target(j, z):
     inner = jnp.where(j == 0, 3, jnp.where(j == 1, 0, jnp.where(j == 2, 2, 1)))
     return jnp.where(z == 0, 3 - j, jnp.where(z == 3, j, jnp.where(z == 1, inner, 3 - inner)))
+
+
+class Part:
+    def __init__(self, ref, base):
+        self.ref, self.base = ref, base
+
+    def __getitem__(self, n):
+        return self.ref[self.base + n]
+
+    def __setitem__(self, n, value):
+        self.ref[self.base + n] = value
+
+
+def parts(ref):
+    bases = (0, CTX * CAP, CTX * CAP + PER * VIS, CTX * CAP + 2 * PER * VIS)
+    return tuple(Part(ref, base) for base in bases)
 
 
 def chosen(blocks_ref, count_ref, dst, src):
@@ -592,8 +608,9 @@
 
 def gather_and_attend(
     blocks_ref, count_ref, len_ref, k_ref, v_ref, q_ref, do_ref,
-    held_0, held_1, picks, place, seen, slot_of, attn_ref, dq_ref, slots_ref, *scratch,
+    held_0, held_1, table_ref, attn_ref, dq_ref, slots_ref, *scratch,
 ):
+    picks, place, seen, slot_of = parts(table_ref)
     _, y, z = coords()
     lists = (blocks_ref, count_ref, len_ref, place, seen, slot_of)
     attention = Attention(0, place, seen, q_ref, do_ref, held_0, attn_ref, dq_ref, slots_ref, scratch[:N_ATTEND])
@@ -636,9 +653,10 @@
 
 
 def attend_and_return(
-    picks, slot_of, place, seen, q_ref, do_ref, held_ref, done_ref,
+    table_ref, q_ref, do_ref, held_ref, done_ref,
     gk_ref, gv_ref, attn_ref, dq_ref, slots_ref, *scratch,
 ):
+    picks, place, seen, slot_of = parts(table_ref)
     _, y, z = coords()
     attention = Attention(1, place, seen, q_ref, do_ref, held_ref, attn_ref, dq_ref, slots_ref, scratch[:N_ATTEND])
     scratch = scratch[N_ATTEND:]
@@ -695,23 +713,23 @@
     keys = key_states.reshape(PER, BLOCK, width)
     values = value_state_rows.reshape(PER, BLOCK, width)
 
-    sizes = (CTX * CAP, PER * VIS, PER * VIS, PER * HELD)
-    _, held_1, picks, place, seen, slot_of, attn_0, dq_0, slots_0 = pl.pallas_call(
+    table = shape((CTX * CAP + 2 * PER * VIS + PER * HELD,), jnp.int32)
+    _, held_1, tables_out, attn_0, dq_0, slots_0 = pl.pallas_call(
         gather_and_attend,
-        out_shape=(held, held) + tuple(shape((n,), jnp.int32) for n in sizes) + (half, half, slots),
+        out_shape=(held, held, table, half, half, slots),
         in_specs=[smem] * 3 + [hbm] * 4,
-        out_specs=(hbm,) * 2 + (smem,) * 4 + (vmem,) * 3,
+        out_specs=(hbm,) * 2 + (smem,) + (vmem,) * 3,
         scratch_shapes=Attention.scratch(tokens, lanes) + 2 * exchange_scratch(sems),
         compiler_params=remote(0, 58),
     )(vis_blocks.T, vis_count, vis_len.T, keys, values, query_states, grad_out)
     grad_key, grad_value, attn_1, dq_1, _ = pl.pallas_call(
         attend_and_return,
         out_shape=(whole, whole, half, half, slots),
-        in_specs=[smem] * 4 + [hbm] * 3 + [vmem],
+        in_specs=[smem] + [hbm] * 3 + [vmem],
         out_specs=(vmem,) * 5,
         scratch_shapes=Attention.scratch(tokens, lanes) + 2 * return_scratch(sems),
         compiler_params=remote(1, 48),
-    )(picks, slot_of, place, seen, query_states, grad_out, held_1, slots_0)
+    )(tables_out, query_states, grad_out, held_1, slots_0)
     attention = jnp.concatenate([attn_0, attn_1], axis=1)
     grad_query = jnp.concatenate([dq_0, dq_1], axis=1)
     return attention, grad_query, grad_key, grad_value

time: 130 us -> 128 us (0.985)
  local copies, waits for them, and re-layouts: 5.44 us -> 3.43 us
    unnamed x16 -> x10, local copies, waits for them, and re-layouts: 5.44 us -> 3.43 us
where the time goes in v8:
time: 128 us
  Pallas kernels  121 us (95%)
  local copies, waits for them, and re-layouts  3.43 us (3%)
  other arithmetic  2.41 us (2%)
    pallas_call x1, Pallas kernels, body(): pl.pallas_call(attend_and_return, out_shape=(whole, whole, half, half, sl...  67.6 us
    pallas_call x1, Pallas kernels, body(): pl.pallas_call(gather_and_attend, out_shape=(held, held, table, half, hal...  53.8 us
    unnamed x10, local copies, waits for them, and re-layouts  3.43 us

profile of v8, /device:TPU:36, one launch (start us, length us, event | category | flops | bytes accessed | tf_op | source)
XLA Modules:
  0.0 127.9 jit_solution(10752596339397610846)
XLA Ops:
  0.6 53.8 %shard_map.102 = (bf16[40,128,256]{2,1,0:T(8,128)(2,1)}, bf16[40,128,256]{2,1,0:T(8,128)(2,1)}, s32[240]{0:T(256)}, bf16[512,1024]{1,0:T(8,128)(2,1)}, bf16[512,...) custom-call(s32[6,64]{1,0:T(8,128)} %bitcast.6, s32[64]{0:T(128)} %count_ref.1, s32[6,64]{1,0:T(8,128)} %bitcast.7, ...), custom_call_target="tpu_custom_call" | custom-call | tf_op jit(solution)/shard_map/pallas_call | solution.py:717
  54.4 0.0 copy-start
  54.4 1.4 %copy-done = bf16[24,128,256]{2,1,0:T(8,128)(2,1)S(1)} copy-done((bf16[24,128,256]{2,1,0:T(8,128)(2,1)S(1)}, bf16[24,128,256]{2,1,0:T(8,128)(2,1)}, u32[]{:S(2)}) %copy-start) | copy-done | bytes 1572888
  55.8 0.0 copy-start.1
  55.8 0.6 copy-done.1
  56.4 0.0 copy-start.2
  56.4 0.0 copy-start.3
  56.4 67.6 %shard_map.103 = (bf16[512,256]{1,0:T(8,128)(2,1)S(1)}, bf16[512,256]{1,0:T(8,128)(2,1)S(1)}, bf16[512,1024]{1,0:T(8,128)(2,1)S(1)}, bf16[512,1024]{1,0:T(8,128)(2,1)S(1)}, bf16[24,128,256]{2,1,0:T(8,128)(2,1)}) custom-call(s32[240]{0:T(256)S(1)} %copy-done.1, bf16[512,2048]{1,0:T(8,128)(2,1)} %q_ref.3, bf16[512,2048]{1,0:T(8,128)(2,1)} %do_ref.3, ...), custom_call_target="tpu_custom_call" | custom-call | tf_op jit(solution)/shard_map/pallas_call | solution.py:725
  124.1 0.0 copy-done.2
  124.1 0.0 copy-done.3
  124.1 2.4 %pad_maximum_fusion = (bf16[512,2048]{1,0:T(8,128)(2,1)}, bf16[512,2048]{1,0:T(8,128)(2,1)}) fusion(bf16[512,1024]{1,0:T(8,128)(2,1)S(1)} %get-tuple-element.17, bf16[512,1024]{1,0:T(8,128)(2,1)S(1)} %copy-done.2, bf16[512,1024]{1,0:T(8,128)(2,1)S(1)} %get-tuple-element.19, bf16[512,1024]{1,0:T(8,128)(2,1)S(1)} %copy-done.3), kind=kLoop, calls=%fused_computation | loop fusion | flops 8388608 | bytes 8388608 | tf_op jit(solution)/shard_map/concatenate | solution.py:733
  126.5 0.7 copy.13
  127.2 0.7 copy.14
Async XLA Ops:
  54.4 1.4 %copy-start = (bf16[24,128,256]{2,1,0:T(8,128)(2,1)S(1)}, bf16[24,128,256]{2,1,0:T(8,128)(2,1)}, u32[]{:S(2)}) copy-start(bf16[24,128,256]{2,1,0:T(8,128)(2,1)} %get-tuple-element.16.done_ref) | copy-start | bytes 4718596
  55.8 0.6 copy-start.1
  56.4 67.6 %copy-start.2 = (bf16[512,1024]{1,0:T(8,128)(2,1)S(1)}, bf16[512,1024]{1,0:T(8,128)(2,1)}, u32[]{:S(2)}) copy-start(bf16[512,1024]{1,0:T(8,128)(2,1)} %get-tuple-element.13) | copy-start | bytes 3145732
  56.4 67.7 %copy-start.3 = (bf16[512,1024]{1,0:T(8,128)(2,1)S(1)}, bf16[512,1024]{1,0:T(8,128)(2,1)}, u32[]{:S(2)}) copy-start(bf16[512,1024]{1,0:T(8,128)(2,1)} %get-tuple-element.18) | copy-start | bytes 3145732
